TPU v7x, 32 devices: a whole 2x2x4 slice. The times are simulated.
32 devices in a mesh: dp: 16 (over z, x, core), mp: 2 (over y).
Axes of the slice: x: 2, y: 2, z: 4, core: 2. Of those that a mesh axis runs over, the one named last changes fastest.
Arguments:
- inputs: bfloat16 [2, 12288, 512], P(None, ('dp', 'mp')), may hold values from -6 to 6
- ff_in: bfloat16 [1, 2, 512, 2048], P(None, None, 'dp', 'mp'), may hold values from -0.25 to 0.25
- ff_out: bfloat16 [1, 2, 2048, 512], P(None, None, 'mp', 'dp'), may hold values from -0.25 to 0.25
- in_mats: bfloat16 [1, 6, 512, 512], P(None, None, 'dp', 'mp'), as said below
- attn_out: bfloat16 [1, 512, 512], P(None, 'mp', 'dp'), as said below
- conv_out: bfloat16 [1, 512, 512], P(None, 'mp', 'dp'), may hold values from -0.25 to 0.25
- dw_kernel: bfloat16 [1, 31, 512], P(None, None, ('mp', 'dp')), may hold values from -1 to 1
- bn_affine: bfloat16 [1, 2, 512], P(None, None, ('mp', 'dp')), may hold values from 0.099609375 to 1.8984375
- pos_bias: bfloat16 [1, 2, 512], P(None, None, ('mp', 'dp')), may hold values from -3 to 3
- ln_gain: float32 [1, 5, 512], P(None, None, ('dp', 'mp')), may hold values from 0.5 to 1.5
- ln_bias: float32 [1, 5, 512], P(None, None, ('dp', 'mp')), may hold values from -2 to 2
- cotangent: bfloat16 [2, 12288, 512], P(None, ('dp', 'mp')), may hold values from -6 to 6
Outputs:
- outputs: float32 [2, 12288, 512], P(None, ('dp', 'mp'))
- input_grad: float32 [2, 12288, 512], P(None, ('dp', 'mp'))
- grad_ff_in: float32 [1, 2, 512, 2048], P(None, None, 'dp', 'mp')
- grad_ff_out: float32 [1, 2, 2048, 512], P(None, None, 'mp', 'dp')
- grad_in_mats: float32 [1, 6, 512, 512], P(None, None, 'dp', 'mp')
- grad_attn_out: float32 [1, 512, 512], P(None, 'mp', 'dp')
- grad_conv_out: float32 [1, 512, 512], P(None, 'mp', 'dp')
- grad_dw_kernel: float32 [1, 31, 512], P(None, None, ('mp', 'dp'))
- grad_bn_affine: float32 [1, 2, 512], P(None, None, ('mp', 'dp'))
- grad_pos_bias: float32 [1, 2, 512], P(None, None, ('mp', 'dp'))
- grad_ln_gain: float32 [1, 5, 512], P(None, None, ('dp', 'mp'))
- grad_ln_bias: float32 [1, 5, 512], P(None, None, ('dp', 'mp'))
Inputs may be any that keep to these rules, and one draw needn't show every extreme that they name: `in_mats`: mean zero, entries of order 512^(-1/2). `attn_out`: mean zero, entries of order (32 / 512)^(1/2).
All inputs are finite; a program needn't handle non-finite values.
Results may differ from a plain program's by a relative error of at most 0.034.
Values may be sent and summed in bfloat16 or wider, within the bound.
A program may use at most 256 MiB of HBM per device.

v0:
```python
import math

import jax
import jax.numpy as jnp
from jax import lax
from jax.sharding import PartitionSpec as P

D = 512
HEADS = 8
HEAD_DIM = 64
LENGTH = 768
LAYERS = 1


epsilon = 1e-05
bfloat = jnp.bfloat16
single = jnp.float32


def relative_table(length, width):
    distance = (length - 1 - jnp.arange(2 * length - 1)).astype(jnp.float32)
    frequency = jnp.exp(
        jnp.arange(width // 2).astype(jnp.float32) * (-2.0 * math.log(10000.0) / width)
    )
    angles = distance[:, None] * frequency[None, :]
    return jnp.concatenate([jnp.sin(angles), jnp.cos(angles)], axis=1)


def relative_shift(band):
    length = band.shape[-2]
    leading = band.shape[:-2]
    flattened = band.reshape(leading + (length * (2 * length - 1),))
    picked = flattened[..., length - 1 : length - 1 + length * (2 * length - 2)]
    return picked.reshape(leading + (length, 2 * length - 2))[..., :length]


def relative_shift_back(grad_scores):
    length = grad_scores.shape[-1]
    leading = grad_scores.shape[:-2]
    spacing = [(0, 0)] * len(leading)
    widened = jnp.pad(grad_scores, spacing + [(0, 0), (0, length - 2)])
    flattened = widened.reshape(leading + (length * (2 * length - 2),))
    flattened = jnp.pad(flattened, spacing + [(length - 1, 1)])
    return flattened.reshape(leading + (length, 2 * length - 1))


def norm_rows(values, gain_row, bias_row):
    center = jnp.mean(values, axis=-1, keepdims=True)
    offset = values - center
    inverse_std = lax.rsqrt(jnp.mean(offset * offset, axis=-1, keepdims=True) + epsilon)
    unit_rows = offset * inverse_std
    return (unit_rows * gain_row + bias_row, (unit_rows, inverse_std))


def norm_rows_back(grad_normed, kept, gain_row, select):
    unit_rows, inverse_std = kept
    grad_unit = grad_normed * gain_row
    grad_values = inverse_std * (
        grad_unit
        - jnp.mean(grad_unit, axis=-1, keepdims=True)
        - unit_rows * jnp.mean(grad_unit * unit_rows, axis=-1, keepdims=True)
    )
    return (
        grad_values,
        jnp.sum(select(grad_normed * unit_rows), axis=0),
        jnp.sum(select(grad_normed), axis=0),
    )


def swish_slope(values):
    sigmoid = jax.nn.sigmoid(values)
    return sigmoid * (1.0 + values * (1.0 - sigmoid))


def depthwise(gated, taps):
    kernel_size = taps.shape[0]
    margin = (kernel_size - 1) // 2
    length = gated.shape[1]
    padded = jnp.pad(gated, ((0, 0), (margin, margin), (0, 0)))
    convolved = jnp.zeros_like(gated)
    for tap_index in range(kernel_size):
        convolved = convolved + taps[tap_index] * padded[:, tap_index : tap_index + length, :]
    return convolved


def depthwise_back(gated, grad_convolved, taps):
    kernel_size = taps.shape[0]
    margin = (kernel_size - 1) // 2
    length = gated.shape[1]
    padded = jnp.pad(gated, ((0, 0), (margin, margin), (0, 0)))
    grad_padded = jnp.pad(grad_convolved, ((0, 0), (margin, margin), (0, 0)))
    grad_gated = jnp.zeros_like(gated)
    grad_taps = []
    for tap_index in range(kernel_size):
        begin = 2 * margin - tap_index
        grad_gated = grad_gated + taps[tap_index] * grad_padded[:, begin : begin + length, :]
        grad_taps.append(
            jnp.sum(padded[:, tap_index : tap_index + length, :] * grad_convolved, axis=(0, 1))
        )
    return (grad_gated, jnp.stack(grad_taps))


def attention_scores(with_content, with_position, key_rows, position):
    content = jnp.einsum("sihd,sjhd->shij", with_content, key_rows, preferred_element_type=single)
    band = jnp.einsum("sihd,rhd->shir", with_position, position, preferred_element_type=single)
    return content + relative_shift(band)


def per_device(
    inputs,
    ff_in,
    ff_out,
    in_mats,
    attn_out,
    conv_out,
    dw_kernel,
    bn_affine,
    pos_bias,
    ln_gain,
    ln_bias,
    cotangent,
):
    model_size = lax.axis_size("mp")
    local_rows = inputs.shape[1]
    group_rows = local_rows * model_size
    sequences = group_rows // LENGTH
    head_count = HEADS // model_size
    score_scale = HEAD_DIM ** (-0.5)
    total_rows = group_rows * lax.axis_size("dp")
    head_shape = (sequences, LENGTH, head_count, HEAD_DIM)
    sinusoid = relative_table(LENGTH, D).astype(bfloat)
    norm_gain, norm_bias = (
        lax.all_gather(ln_gain, ("dp", "mp"), axis=2, tiled=True),
        lax.all_gather(ln_bias, ("dp", "mp"), axis=2, tiled=True),
    )

    def spread(local_values):
        return lax.all_gather(local_values, "mp", axis=0, tiled=True)

    def spread_grad(local_values):
        return lax.all_gather(local_values, "mp", axis=0, tiled=True)

    def reduce_out(term_fn):
        return lax.psum_scatter(
            term_fn(jnp.int32(0), local_rows * lax.axis_size("mp")).astype(jnp.bfloat16),
            "mp",
            scatter_dimension=0,
            tiled=True,
        ).astype(jnp.float32)

    def reduce_grad(term_fn):
        return lax.psum_scatter(
            term_fn(jnp.int32(0), local_rows * lax.axis_size("mp")).astype(jnp.bfloat16),
            "mp",
            scatter_dimension=0,
            tiled=True,
        ).astype(jnp.float32)

    def own_rows(values):
        return values

    entered_inputs, entered_cotangent = (inputs, cotangent)

    def norm_input(values, layer_index, slot_index):
        normed, kept = norm_rows(
            values, norm_gain[layer_index, slot_index], norm_bias[layer_index, slot_index]
        )
        return (spread(normed.astype(bfloat)), kept)

    def ff_forward(full_rows, w_first, w_second):
        hidden_pre = jnp.dot(full_rows, w_first, preferred_element_type=single)
        hidden = jax.nn.silu(hidden_pre).astype(bfloat)

        def row_term(first_row, row_count):
            return jnp.dot(hidden, w_second, preferred_element_type=single)

        return (reduce_out(row_term), (hidden_pre, hidden))

    def ff_backward(grad_local, full_rows, kept, w_first, w_second):
        hidden_pre, hidden = kept
        grad_full = spread_grad(grad_local)
        grad_second = jnp.einsum("gf,gd->fd", hidden, grad_full, preferred_element_type=single)
        grad_hidden = jnp.einsum("gd,fd->gf", grad_full, w_second, preferred_element_type=single)
        grad_pre = (grad_hidden * swish_slope(hidden_pre)).astype(bfloat)
        grad_first = jnp.einsum("gd,gf->df", full_rows, grad_pre, preferred_element_type=single)

        def row_term(first_row, row_count):
            return jnp.einsum("gf,df->gd", grad_pre, w_first, preferred_element_type=single)

        return (reduce_grad(row_term), grad_first, grad_second)

    def attention_forward(full_rows, matrices, w_attn, biases):
        projected = jnp.einsum(
            "gd,kdc->kgc", full_rows, matrices[0:3], preferred_element_type=single
        )
        query_rows = projected[0].reshape(head_shape)
        key_rows = projected[1].astype(bfloat).reshape(head_shape)
        value_rows = projected[2].astype(bfloat).reshape(head_shape)
        bias_pair = biases.astype(single).reshape(2, head_count, HEAD_DIM)
        with_content = (score_scale * (query_rows + bias_pair[0])).astype(bfloat)
        with_position = (score_scale * (query_rows + bias_pair[1])).astype(bfloat)
        position = (
            jnp.dot(sinusoid, matrices[3], preferred_element_type=single)
            .astype(bfloat)
            .reshape(2 * LENGTH - 1, head_count, HEAD_DIM)
        )
        scores = attention_scores(with_content, with_position, key_rows, position)
        row_max = jnp.max(scores, axis=-1, keepdims=True)
        exponent = jnp.exp(scores - row_max)
        row_total = jnp.sum(exponent, axis=-1, keepdims=True)
        weights_low = (exponent / row_total).astype(bfloat)
        log_total = row_max + jnp.log(row_total)
        context = jnp.einsum(
            "shij,sjhd->sihd", weights_low, value_rows, preferred_element_type=single
        )
        context = context.astype(bfloat).reshape(group_rows, head_count * HEAD_DIM)

        def row_term(first_row, row_count):
            return jnp.dot(context, w_attn, preferred_element_type=single)

        return (
            reduce_out(row_term),
            (with_content, with_position, key_rows, value_rows, position, log_total, context),
        )

    def attention_backward(grad_local, full_rows, kept, matrices, w_attn):
        with_content, with_position, key_rows, value_rows, position, log_total, context = kept
        grad_full = spread_grad(grad_local)
        grad_attn = jnp.einsum("gc,gd->cd", context, grad_full, preferred_element_type=single)
        grad_context = (
            jnp.einsum("gd,cd->gc", grad_full, w_attn, preferred_element_type=single)
            .astype(bfloat)
            .reshape(head_shape)
        )
        scores = attention_scores(with_content, with_position, key_rows, position)
        probs_full = jnp.exp(scores - log_total)
        grad_probs = jnp.einsum(
            "sihd,sjhd->shij", grad_context, value_rows, preferred_element_type=single
        )
        grad_value = jnp.einsum(
            "shij,sihd->sjhd",
            probs_full.astype(bfloat),
            grad_context,
            preferred_element_type=single,
        )
        grad_scores = (
            probs_full * (grad_probs - jnp.sum(probs_full * grad_probs, axis=-1, keepdims=True))
        ).astype(bfloat)
        grad_content = jnp.einsum(
            "shij,sjhd->sihd", grad_scores, key_rows, preferred_element_type=single
        )
        grad_key = jnp.einsum(
            "shij,sihd->sjhd", grad_scores, with_content, preferred_element_type=single
        )
        grad_band = relative_shift_back(grad_scores)
        grad_posq = jnp.einsum("shir,rhd->sihd", grad_band, position, preferred_element_type=single)
        grad_position = jnp.einsum(
            "shir,sihd->srhd", grad_band, with_position, preferred_element_type=single
        )
        grad_position = grad_position.astype(bfloat).reshape(
            sequences, 2 * LENGTH - 1, head_count * HEAD_DIM
        )
        grad_pos_matrix = jnp.einsum(
            "rk,src->kc", sinusoid, grad_position, preferred_element_type=single
        )
        grad_query = (
            (score_scale * (grad_content + grad_posq)).astype(bfloat).reshape(group_rows, -1)
        )
        grad_bias = score_scale * jnp.stack(
            [jnp.sum(grad_content, axis=(0, 1)), jnp.sum(grad_posq, axis=(0, 1))]
        ).reshape(2, -1)
        stacked_grad = jnp.stack(
            [
                grad_query,
                grad_key.astype(bfloat).reshape(group_rows, -1),
                grad_value.astype(bfloat).reshape(group_rows, -1),
            ]
        )
        grad_proj = jnp.einsum(
            "gd,kgc->kdc", full_rows, stacked_grad, preferred_element_type=single
        )

        def row_term(first_row, row_count):
            return jnp.einsum(
                "kgc,kdc->gd", stacked_grad, matrices[0:3], preferred_element_type=single
            )

        return (reduce_grad(row_term), grad_proj, grad_pos_matrix, grad_attn, grad_bias)

    def conv_backward(grad_local, full_rows, kept, matrices, w_conv, kernel, affine):
        linear_part, gate_part, gated, unit_values, inverse_std, scaled, active = kept
        grad_full = spread_grad(grad_local)
        grad_conv = jnp.einsum("gc,gd->cd", active, grad_full, preferred_element_type=single)
        grad_active = jnp.einsum(
            "gd,cd->gc", grad_full, w_conv, preferred_element_type=single
        ).reshape(sequences, LENGTH, -1)
        grad_scaled = grad_active * swish_slope(scaled)
        local_shift = jnp.sum(grad_scaled, axis=(0, 1))
        local_scale = jnp.sum(grad_scaled * unit_values, axis=(0, 1))
        sum_shift, sum_scale = lax.psum((local_shift, local_scale), "dp")
        scale_shift = affine.astype(single)
        grad_convolved = (
            scale_shift[0]
            * inverse_std
            * (grad_scaled - sum_shift / total_rows - unit_values * (sum_scale / total_rows))
        )
        grad_gated, grad_taps = depthwise_back(gated, grad_convolved, kernel.astype(single))
        grad_gated = grad_gated.reshape(group_rows, -1)
        sigmoid = jax.nn.sigmoid(gate_part)
        grad_linear = (grad_gated * sigmoid).astype(bfloat)
        grad_gate = (grad_gated * linear_part * sigmoid * (1.0 - sigmoid)).astype(bfloat)
        stacked_grad = jnp.stack([grad_linear, grad_gate])
        grad_proj = jnp.einsum(
            "gd,kgc->kdc", full_rows, stacked_grad, preferred_element_type=single
        )

        def row_term(first_row, row_count):
            return jnp.einsum(
                "kgc,kdc->gd", stacked_grad, matrices[4:6], preferred_element_type=single
            )

        return (
            reduce_grad(row_term),
            grad_proj,
            grad_conv,
            grad_taps,
            jnp.stack([local_scale, local_shift]),
        )

    def layer_backward(grad_result, kept, weights, layer_index):
        w_in, w_out, matrices, w_attn, w_conv, kernel, affine, biases = weights
        (
            full_one,
            norm_one,
            ff_first,
            full_two,
            norm_two,
            attn_kept,
            full_three,
            norm_three,
            conv_kept,
            full_four,
            norm_four,
            ff_second,
            norm_five,
        ) = kept
        gains = [None] * 5
        shifts = [None] * 5
        grad_four, gains[4], shifts[4] = norm_rows_back(
            grad_result, norm_five, norm_gain[layer_index, 4], own_rows
        )
        scattered, first_two, second_two = ff_backward(
            (0.5 * grad_four).astype(bfloat), full_four, ff_second, w_in[1], w_out[1]
        )
        grad_norm, gains[3], shifts[3] = norm_rows_back(
            scattered, norm_four, norm_gain[layer_index, 3], own_rows
        )
        grad_three = grad_four + grad_norm
        scattered, conv_proj, grad_conv, grad_taps, grad_affine = conv_backward(
            grad_three.astype(bfloat), full_three, conv_kept, matrices, w_conv, kernel, affine
        )
        grad_norm, gains[2], shifts[2] = norm_rows_back(
            scattered, norm_three, norm_gain[layer_index, 2], own_rows
        )
        grad_two = grad_three + grad_norm
        scattered, attn_proj, grad_pos_matrix, grad_attn, grad_bias = attention_backward(
            grad_two.astype(bfloat), full_two, attn_kept, matrices, w_attn
        )
        grad_norm, gains[1], shifts[1] = norm_rows_back(
            scattered, norm_two, norm_gain[layer_index, 1], own_rows
        )
        grad_one = grad_two + grad_norm
        scattered, first_one, second_one = ff_backward(
            (0.5 * grad_one).astype(bfloat), full_one, ff_first, w_in[0], w_out[0]
        )
        grad_norm, gains[0], shifts[0] = norm_rows_back(
            scattered, norm_one, norm_gain[layer_index, 0], own_rows
        )
        grad_zero = grad_one + grad_norm
        pieces = (
            jnp.stack([first_one, first_two]),
            jnp.stack([second_one, second_two]),
            jnp.concatenate([attn_proj, grad_pos_matrix[None], conv_proj], axis=0),
            grad_attn,
            grad_conv,
            grad_taps,
            grad_affine,
            grad_bias,
            jnp.stack(gains),
            jnp.stack(shifts),
        )
        return (grad_zero, pieces)

    accumulated = [None] * LAYERS
    output_list = []
    input_list = []
    for micro_index in range(inputs.shape[0]):
        values = entered_inputs[micro_index].astype(single)
        layer_index = 0
        layer_w_in = lax.all_gather(ff_in[layer_index], "dp", axis=1, tiled=True)
        layer_w_out = lax.all_gather(ff_out[layer_index], "dp", axis=2, tiled=True)
        layer_matrices = lax.all_gather(in_mats[layer_index], "dp", axis=1, tiled=True)
        layer_w_attn = lax.all_gather(attn_out[layer_index], "dp", axis=1, tiled=True)
        layer_w_conv = lax.all_gather(conv_out[layer_index], "dp", axis=1, tiled=True)
        layer_kernel = lax.all_gather(dw_kernel[layer_index], "dp", axis=1, tiled=True)
        layer_affine = lax.all_gather(bn_affine[layer_index], "dp", axis=1, tiled=True)
        layer_biases = lax.all_gather(pos_bias[layer_index], "dp", axis=1, tiled=True)
        layer_full_one, layer_norm_one = norm_input(values, layer_index, 0)
        branch, layer_ff_first = ff_forward(layer_full_one, layer_w_in[0], layer_w_out[0])
        after_one = values + 0.5 * branch
        layer_full_two, layer_norm_two = norm_input(after_one, layer_index, 1)
        branch, layer_attn_kept = attention_forward(
            layer_full_two, layer_matrices, layer_w_attn, layer_biases
        )
        after_two = after_one + branch
        layer_full_three, layer_norm_three = norm_input(after_two, layer_index, 2)
        conv_w_conv = layer_w_conv
        conv_projected = jnp.einsum(
            "gd,kdc->kgc", layer_full_three, layer_matrices[4:6], preferred_element_type=single
        )
        conv_linear_part = conv_projected[0]
        conv_gate_part = conv_projected[1]
        conv_gated = (conv_linear_part * jax.nn.sigmoid(conv_gate_part)).reshape(
            sequences, LENGTH, -1
        )
        taps = layer_kernel.astype(single)
        conv_convolved = depthwise(conv_gated, taps)
        total_sum = lax.psum(jnp.sum(conv_convolved, axis=(0, 1)), "dp")
        center = total_sum / total_rows
        offset = conv_convolved - center
        variance = lax.psum(jnp.sum(offset * offset, axis=(0, 1)), "dp") / total_rows
        conv_inverse_std = lax.rsqrt(variance + epsilon)
        conv_unit_values = (conv_convolved - center) * conv_inverse_std
        conv_scale_shift = layer_affine.astype(single)
        conv_scaled = conv_unit_values * conv_scale_shift[0] + conv_scale_shift[1]
        conv_active = jax.nn.silu(conv_scaled).astype(bfloat).reshape(group_rows, -1)

        def conv_row_term(first_row, row_count):
            return jnp.dot(conv_active, conv_w_conv, preferred_element_type=single)

        branch = reduce_out(conv_row_term)
        layer_conv_kept = (
            conv_linear_part,
            conv_gate_part,
            conv_gated,
            conv_unit_values,
            conv_inverse_std,
            conv_scaled,
            conv_active,
        )
        after_three = after_two + branch
        layer_full_four, layer_norm_four = norm_input(after_three, layer_index, 3)
        branch, layer_ff_second = ff_forward(layer_full_four, layer_w_in[1], layer_w_out[1])
        after_four = after_three + 0.5 * branch
        result, layer_norm_five = norm_rows(
            after_four, norm_gain[layer_index, 4], norm_bias[layer_index, 4]
        )
        layer_kept = (
            layer_full_one,
            layer_norm_one,
            layer_ff_first,
            layer_full_two,
            layer_norm_two,
            layer_attn_kept,
            layer_full_three,
            layer_norm_three,
            layer_conv_kept,
            layer_full_four,
            layer_norm_four,
            layer_ff_second,
            layer_norm_five,
        )
        values = result
        kept = layer_kept
        kept_layers = [kept]
        output_list.append(own_rows(values))
        grad_values = entered_cotangent[micro_index].astype(single)
        for layer_index in reversed(range(LAYERS)):
            grad_values, pieces = layer_backward(
                grad_values,
                kept_layers[layer_index],
                (
                    lax.all_gather(ff_in[layer_index], "dp", axis=1, tiled=True),
                    lax.all_gather(ff_out[layer_index], "dp", axis=2, tiled=True),
                    lax.all_gather(in_mats[layer_index], "dp", axis=1, tiled=True),
                    lax.all_gather(attn_out[layer_index], "dp", axis=1, tiled=True),
                    lax.all_gather(conv_out[layer_index], "dp", axis=1, tiled=True),
                    lax.all_gather(dw_kernel[layer_index], "dp", axis=1, tiled=True),
                    lax.all_gather(bn_affine[layer_index], "dp", axis=1, tiled=True),
                    lax.all_gather(pos_bias[layer_index], "dp", axis=1, tiled=True),
                ),
                layer_index,
            )
            if accumulated[layer_index] is None:
                accumulated[layer_index] = pieces
            else:
                accumulated[layer_index] = jax.tree.map(jnp.add, accumulated[layer_index], pieces)
        input_list.append(own_rows(grad_values))
    stacked_grads = [jnp.stack([accumulated[0][piece_index]]) for piece_index in range(10)]
    weight_grads = (
        lax.psum_scatter(
            stacked_grads[0].astype(jnp.bfloat16), "dp", scatter_dimension=2, tiled=True
        ).astype(jnp.float32),
        lax.psum_scatter(
            stacked_grads[1].astype(jnp.bfloat16), "dp", scatter_dimension=3, tiled=True
        ).astype(jnp.float32),
        lax.psum_scatter(
            stacked_grads[2].astype(jnp.bfloat16), "dp", scatter_dimension=2, tiled=True
        ).astype(jnp.float32),
        lax.psum_scatter(
            stacked_grads[3].astype(jnp.bfloat16), "dp", scatter_dimension=2, tiled=True
        ).astype(jnp.float32),
        lax.psum_scatter(
            stacked_grads[4].astype(jnp.bfloat16), "dp", scatter_dimension=2, tiled=True
        ).astype(jnp.float32),
        lax.psum_scatter(
            stacked_grads[5].astype(jnp.bfloat16), "dp", scatter_dimension=2, tiled=True
        ).astype(jnp.float32),
        lax.psum_scatter(
            stacked_grads[6].astype(jnp.bfloat16), "dp", scatter_dimension=2, tiled=True
        ).astype(jnp.float32),
        lax.psum_scatter(
            stacked_grads[7].astype(jnp.bfloat16), "dp", scatter_dimension=2, tiled=True
        ).astype(jnp.float32),
    )
    norm_grads = (
        lax.psum_scatter(stacked_grads[8], ("dp", "mp"), scatter_dimension=2, tiled=True),
        lax.psum_scatter(stacked_grads[9], ("dp", "mp"), scatter_dimension=2, tiled=True),
    )
    return (
        jnp.stack(output_list),
        jnp.stack(input_list),
        weight_grads[0],
        weight_grads[1],
        weight_grads[2],
        weight_grads[3],
        weight_grads[4],
        weight_grads[5],
        weight_grads[6],
        weight_grads[7],
        norm_grads[0],
        norm_grads[1],
    )


def solution(mesh):
    placed = (
        P(None, ("dp", "mp"), None),
        P(None, None, "dp", "mp"),
        P(None, None, "mp", "dp"),
        P(None, None, "dp", "mp"),
        P(None, "mp", "dp"),
        P(None, "mp", "dp"),
        P(None, None, ("mp", "dp")),
        P(None, None, ("mp", "dp")),
        P(None, None, ("mp", "dp")),
        P(None, None, ("dp", "mp")),
        P(None, None, ("dp", "mp")),
        P(None, ("dp", "mp"), None),
    )
    return jax.shard_map(
        per_device,
        mesh=mesh,
        in_specs=placed,
        out_specs=(
            P(None, ("dp", "mp"), None),
            P(None, ("dp", "mp"), None),
            P(None, None, "dp", "mp"),
            P(None, None, "mp", "dp"),
            P(None, None, "dp", "mp"),
            P(None, "mp", "dp"),
            P(None, "mp", "dp"),
            P(None, None, ("mp", "dp")),
            P(None, None, ("mp", "dp")),
            P(None, None, ("mp", "dp")),
            P(None, None, ("dp", "mp")),
            P(None, None, ("dp", "mp")),
        ),
        check_vma=False,
    )
```

profile of v0, /device:TPU:0, one launch (start us, length us, event | category | flops | bytes accessed | tf_op | source)
XLA Modules:
  0.0 2229.2 jit_solution(543761326474956931)
XLA Ops:
  10.2 71.6 %all_gather.101 = f32[1,5,512]{1,0,2:T(1,128)S(1)} all-gather(f32[1,5,16]{1,0,2:T(1,128)S(1)} %copy.136), channel_id=1, replica_groups=mesh['dp'=16,'mp'=2] {'dp','mp'}, dimensions={2}, use_global_device_ids=true | all-gather | bytes 10560 | tf_op jit(solution)/shard_map/all_gather | solution.py:134
  81.9 64.9 %all_gather.100 = f32[1,5,512]{1,0,2:T(1,128)S(1)} all-gather(f32[1,5,16]{1,0,2:T(1,128)S(1)} %copy.135), channel_id=1, replica_groups=mesh['dp'=16,'mp'=2] {'dp','mp'}, dimensions={2}, use_global_device_ids=true | all-gather | bytes 10560 | tf_op jit(solution)/shard_map/all_gather | solution.py:133
  186.7 14.7 reduce-scatter.34.cloned.1.call-done
  203.0 11.5 all_gather.114
  222.3 22.1 all-gather.3
  248.3 18.6 all-gather.4
  280.6 12.0 all_gather.105
  292.6 11.2 all_gather.115
  314.7 18.7 copy.139
  333.3 28.5 %reshape.2366 = f32[4715520]{0:T(1024)} reshape(f32[1,4,768,1535]{3,2,1,0:T(8,128)} %copy.139) | data formatting | bytes 37724160
  361.9 23.6 %reshape.2174 = f32[1,4,1178880]{2,1,0:T(4,128)} reshape(f32[4715520]{0:T(1024)} %reshape.2366) | data formatting | bytes 37724160 | tf_op jit(solution)/shard_map/reshape | solution.py:32
  385.4 20.4 slice.1029
  405.9 54.0 %reshape.2368 = f32[4712448]{0:T(1024)} reshape(f32[1,4,1178112]{2,1,0:T(4,128)} %slice.1029) | data formatting | bytes 37699584
  459.9 18.7 reshape.2175
  486.7 9.8 copy.207
  516.6 18.7 copy.143
  535.3 28.5 %reshape.2362 = f32[4715520]{0:T(1024)} reshape(f32[1,4,768,1535]{3,2,1,0:T(8,128)} %copy.143) | data formatting | bytes 37724160
  563.9 23.6 %reshape.2179 = f32[1,4,1178880]{2,1,0:T(4,128)} reshape(f32[4715520]{0:T(1024)} %reshape.2362) | data formatting | bytes 37724160 | tf_op jit(solution)/shard_map/reshape | solution.py:32
  587.4 20.6 slice.1078
  608.1 53.8 %reshape.2364 = f32[4712448]{0:T(1024)} reshape(f32[1,4,1178112]{2,1,0:T(4,128)} %slice.1078) | data formatting | bytes 37699584
  661.9 18.7 reshape.2180
  688.6 9.9 copy.208
  711.4 19.2 all-gather.5
  730.6 17.8 all-gather.6
  748.6 19.5 all-gather.7
  778.1 12.0 all_gather.110
  790.2 11.2 all_gather.116
  812.8 29.5 %all-reduce.13 = (f32[256]{0:T(256)S(1)}, f32[256]{0:T(256)S(1)}) all-reduce(f32[256]{0:T(256)S(1)} %get-tuple-element.258, f32[256]{0:T(256)S(1)} %get-tuple-element.256), channel_id=1, replica_groups=mesh['dp'=16,'mp'=2] {'dp'}, use_global_device_ids=true, to_apply=%region_11.12 | all-reduce | flops 512 | bytes 4096 | tf_op jit(solution)/shard_map/psum | solution.py:428
  842.6 29.5 %all-reduce.12 = (f32[256]{0:T(256)S(1)}, f32[256]{0:T(256)S(1)}) all-reduce(f32[256]{0:T(256)S(1)} %multiply_reduce_fusion.71, f32[256]{0:T(256)S(1)} %multiply_reduce_fusion.66), channel_id=1, replica_groups=mesh['dp'=16,'mp'=2] {'dp'}, use_global_device_ids=true, to_apply=%region_13.14 | all-reduce | flops 512 | bytes 4096 | tf_op jit(solution)/shard_map/psum | solution.py:431
  878.0 11.6 reduce-scatter.38.cloned.1.call-done
  891.7 17.8 reduce-scatter.46.cloned.1.call-done
  912.1 11.5 all_gather.117
  929.7 15.2 all_gather.113
  955.8 14.2 reduce-scatter.40.cloned.1.call-done
  977.1 11.5 all_gather.118
  993.5 15.7 all_gather.122
  1019.4 14.4 reduce-scatter.58.cloned.1.call-done
  1040.6 11.5 all_gather.123
  1052.1 10.6 all_gather.119
  1067.4 31.9 %all-reduce.11 = (f32[256]{0:T(256)S(1)}, f32[256]{0:T(256)S(1)}, f32[256]{0:T(256)S(1)}, f32[256]{0:T(256)S(1)}) all-reduce(f32[256]{0:T(256)S(1)} %get-tuple-element.153, f32[256]{0:T(256)S(1)} %get-tuple-element.152, f32[256]{0:T(256)S(1)} %get-tuple-element.155, ...), channel_id=1, replica_groups=mesh['dp'=16,'mp'=2] {'dp'}, use_global_device_ids=true, to_apply=%region_48.49 | all-reduce | flops 1024 | bytes 8192 | tf_op jit(solution)/shard_map/psum | solution.py:300
  1099.4 10.4 multiply_reduce_fusion.31
  1136.9 15.1 reduce-scatter.60.cloned.1.call-done
  1155.5 11.5 all_gather.120
  1178.4 10.2 fusion.2
  1202.3 10.8 all_gather.124
  1236.8 16.8 reshape.2374
  1253.6 13.8 reshape.2187
  1277.0 24.0 %reshape.2376 = bf16[4715520]{0:T(1024)(128)(2,1)} reshape(bf16[1,4,1178880]{2,1,0:T(4,128)(2,1)} %pad.33) | data formatting | bytes 18862080
  1301.0 18.9 reshape.2188
  1333.9 10.4 fusion
  1362.8 16.8 reshape.2370
  1379.6 13.8 reshape.2193
  1403.0 24.1 %reshape.2372 = bf16[4715520]{0:T(1024)(128)(2,1)} reshape(bf16[1,4,1178880]{2,1,0:T(4,128)(2,1)} %pad.36) | data formatting | bytes 18862080
  1427.0 18.8 reshape.2194
  1464.7 12.7 reduce-scatter.62.cloned.1.call-done
  1483.5 11.7 all_gather.121
  1506.4 18.4 all_gather.125
  1637.3 29.3 %reduce-scatter.70.cloned.1.call-done = bf16[16,31]{1,0:T(8,128)(2,1)} async-done(((bf16[256,31]{1,0:T(8,128)(2,1)}), bf16[16,31]{1,0:T(8,128)(2,1)}) %reduce-scatter.70.cloned.1.call-update) | async-done | bytes 1008
  1668.1 52.9 %reduce-scatter.74.cloned.1.call-done = bf16[16,2]{1,0:T(8,128)(2,1)} async-done(((bf16[256,2]{1,0:T(8,128)(2,1)}), bf16[16,2]{1,0:T(8,128)(2,1)}) %reduce-scatter.74.cloned.1.call-update) | async-done | bytes 80
  1722.4 63.5 %reduce-scatter.68.cloned.1.call-done = bf16[1,6,32,256]{3,1,0,2:T(8,128)(2,1)} async-done(((bf16[1,6,512,256]{3,1,0,2:T(8,128)(2,1)}), bf16[1,6,32,256]{3,1,0,2:T(8,128)(2,1)}) %reduce-scatter.68.cloned.1.call-update) | async-done | bytes 98320 | tf_op jit(solution)/shard_map/reduce_scatter | solution.py:507
  1787.5 105.1 %all-reduce.17.cloned.1.call-done = (bf16[1,2,1024,512]{2,1,0,3:T(2,128)(2,1)}, bf16[1,256,512]{1,0,2:T(2,128)(2,1)}, bf16[1,256,512]{1,0,2:T(2,128)(2,1)}) async-done(((bf16[1,2,1024,512]{2,1,0,3:T(2,128)(2,1)}, bf16[1,256,512]{1,0,2:T(2,128)(2,1)}, bf16[1,256,512]{1,0,2:T(2,128)(2,1)}), (bf16[1,2,1024,512]{2,1,0,3:T(2,128)(2,1)}, bf16[1,256,512]{1,0,2:T(2,128)(2,1)}, ...) | async-done | bytes 2621456
  1902.9 124.2 %reduce-scatter.78.cloned.1.call-done = f32[16,5]{1,0:T(8,128)} async-done(((f32[512,5]{1,0:T(8,128)}), f32[16,5]{1,0:T(8,128)}) %reduce-scatter.78.cloned.1.call-update) | async-done | bytes 336
  2028.6 130.6 %reduce-scatter.76.cloned.1.call-done = f32[16,5]{1,0:T(8,128)} async-done(((f32[512,5]{1,0:T(8,128)}), f32[16,5]{1,0:T(8,128)}) %reduce-scatter.76.cloned.1.call-update) | async-done | bytes 336
  2160.7 59.6 %reduce-scatter.66.cloned.1.call-done = bf16[1,2,32,1024]{3,2,1,0:T(8,128)(2,1)} async-done(((bf16[1,2,512,1024]{3,2,1,0:T(8,128)(2,1)}), bf16[1,2,32,1024]{3,2,1,0:T(8,128)(2,1)}) %reduce-scatter.66.cloned.1.call-update) | async-done | bytes 131088 | tf_op jit(solution)/shard_map/reduce_scatter | solution.py:501
  (950 shorter events, 507.4 us)
Async XLA Ops:
  7.2 161.5 %copy-start.2 = (bf16[2,384,512]{2,1,0:T(8,128)(2,1)S(1)}, bf16[2,384,512]{2,1,0:T(8,128)(2,1)}, u32[]{:S(2)}) copy-start(bf16[2,384,512]{2,1,0:T(8,128)(2,1)} %param.12) | copy-start | bytes 2359300
  7.2 170.7 %all-gather.12.cloned.1.call-start = ((), (), s32[]{:S(2)}) async-start(), calls=%async_computation.41 | async-start | bytes 2228224 | tf_op jit(solution)/shard_map/all_gather | solution.py:400
  7.9 174.4 %all-gather.14.cloned.1.call-start = ((), (), s32[]{:S(2)}) async-start(), calls=%async_computation.42 | async-start | bytes 2228224 | tf_op jit(solution)/shard_map/all_gather | solution.py:401
  8.7 192.7 %reduce-scatter.34.cloned.1.call-start = ((), (), s32[]{:S(2)}) async-start(), calls=%async_computation.23 | async-start | bytes 1179648 | tf_op jit(solution)/shard_map/reduce_scatter | solution.py:144
  168.7 110.4 %copy-start.154 = (f32[512]{0:T(512)}, f32[512]{0:T(512)S(1)}, u32[]{:S(2)}) copy-start(f32[512]{0:T(512)S(1)} %get-tuple-element.181) | copy-start | bytes 6148
  186.1 87.8 %all-gather.16.cloned.1.call-start = ((), (), s32[]{:S(2)}) async-start(), calls=%async_computation.43 | async-start | bytes 1671168 | tf_op jit(solution)/shard_map/all_gather | solution.py:402
  186.7 89.4 %reduce-scatter.42.cloned.1.call-start = ((), (), s32[]{:S(2)}) async-start(), calls=%async_computation.27 | async-start | bytes 1179648 | tf_op jit(solution)/shard_map/reduce_scatter | solution.py:144
  222.1 553.2 %reduce-scatter.36.cloned.1.call-start = ((), (), s32[]{:S(2)}) async-start(), calls=%async_computation.24 | async-start | bytes 1179648 | tf_op jit(solution)/shard_map/reduce_scatter | solution.py:144
  222.3 53.7 %copy-start.16 = (bf16[384,512]{1,0:T(8,128)(2,1)S(1)}, bf16[384,512]{1,0:T(8,128)(2,1)}, u32[]{:S(2)}) copy-start(bf16[384,512]{1,0:T(8,128)(2,1)} %reduce-scatter.34.cloned.1.call-done) | copy-start | bytes 1179652
  248.2 450.3 %copy-start.138 = (f32[4,64]{1,0:T(4,128)}, f32[4,64]{1,0:T(4,128)S(1)}, u32[]{:S(2)}) copy-start(f32[4,64]{1,0:T(4,128)S(1)} %add.909) | copy-start | bytes 3076
  248.3 260.2 %copy-start.93 = (f32[4,64]{1,0:T(4,128)}, f32[4,64]{1,0:T(4,128)S(1)}, u32[]{:S(2)}) copy-start(f32[4,64]{1,0:T(4,128)S(1)} %add.912) | copy-start | bytes 3076
  266.9 442.3 %copy-start.41 = (bf16[1,256,512]{1,2,0:T(8,128)(2,1)}, bf16[1,256,512]{1,2,0:T(8,128)(2,1)S(1)}, u32[]{:S(2)}) copy-start(bf16[1,256,512]{1,2,0:T(8,128)(2,1)S(1)} %all-gather.4) | copy-start | bytes 786436
  276.0 232.6 %copy-start.9 = (bf16[1535,256]{0,1:T(8,128)(2,1)}, bf16[1535,256]{0,1:T(8,128)(2,1)S(1)}, u32[]{:S(2)}) copy-start(bf16[1535,256]{0,1:T(8,128)(2,1)S(1)} %convolution_convert_fusion.2) | copy-start | bytes 2357764
  305.7 392.8 %copy-start.5 = (f32[1,768,256]{1,2,0:T(8,128)}, f32[1,768,256]{1,2,0:T(8,128)S(1)}, u32[]{:S(2)}) copy-start(f32[1,768,256]{1,2,0:T(8,128)S(1)} %slice.1076) | copy-start | bytes 2359300
  306.6 189.8 %copy-start.45 = (bf16[1,768,256]{1,2,0:T(8,128)(2,1)}, bf16[1,768,256]{1,2,0:T(8,128)(2,1)S(1)}, u32[]{:S(2)}) copy-start(bf16[1,768,256]{1,2,0:T(8,128)(2,1)S(1)} %get-tuple-element.266) | copy-start | bytes 1179652
  306.6 196.3 %copy-start.71 = (bf16[1,768,256]{1,2,0:T(8,128)(2,1)}, bf16[1,768,256]{1,2,0:T(8,128)(2,1)S(1)}, u32[]{:S(2)}) copy-start(bf16[1,768,256]{1,2,0:T(8,128)(2,1)S(1)} %get-tuple-element.267) | copy-start | bytes 1179652
  306.7 189.8 %copy-start.7 = (f32[1,768,256]{1,2,0:T(8,128)}, f32[1,768,256]{1,2,0:T(8,128)S(1)}, u32[]{:S(2)}) copy-start(f32[1,768,256]{1,2,0:T(8,128)S(1)} %slice.1024) | copy-start | bytes 2359300
  508.5 266.9 %reduce-scatter.44.cloned.1.call-start = ((), (), s32[]{:S(2)}) async-start(), calls=%async_computation.28 | async-start | bytes 1179648 | tf_op jit(solution)/shard_map/reduce_scatter | solution.py:144
  711.2 64.1 %copy-start.3 = (bf16[2,384,512]{2,1,0:T(8,128)(2,1)S(1)}, bf16[2,384,512]{2,1,0:T(8,128)(2,1)}, u32[]{:S(2)}) copy-start(bf16[2,384,512]{2,1,0:T(8,128)(2,1)} %param.12) | copy-start | bytes 2359300
  711.3 64.1 %copy-start.17 = (bf16[384,512]{1,0:T(8,128)(2,1)S(1)}, bf16[384,512]{1,0:T(8,128)(2,1)}, u32[]{:S(2)}) copy-start(bf16[384,512]{1,0:T(8,128)(2,1)} %reduce-scatter.34.cloned.1.call-done) | copy-start | bytes 1179652
  711.3 64.1 %copy-start.19 = (bf16[384,512]{1,0:T(8,128)(2,1)S(1)}, bf16[384,512]{1,0:T(8,128)(2,1)}, u32[]{:S(2)}) copy-start(bf16[384,512]{1,0:T(8,128)(2,1)} %reduce-scatter.42.cloned.1.call-done) | copy-start | bytes 1179652
  711.3 178.4 %reduce-scatter.38.cloned.1.call-start = ((), (), s32[]{:S(2)}) async-start(), calls=%async_computation.25 | async-start | bytes 1179648 | tf_op jit(solution)/shard_map/reduce_scatter | solution.py:144
  768.1 107.8 %copy-start.110 = (bf16[1,256,512]{1,2,0:T(8,128)(2,1)}, bf16[1,256,512]{1,2,0:T(8,128)(2,1)S(1)}, u32[]{:S(2)}) copy-start(bf16[1,256,512]{1,2,0:T(8,128)(2,1)S(1)} %all-gather.7) | copy-start | bytes 786436
  808.7 67.2 %copy-start.29 = (f32[1,768,256]{2,1,0:T(8,128)}, f32[1,768,256]{2,1,0:T(8,128)S(1)}, u32[]{:S(2)}) copy-start(f32[1,768,256]{2,1,0:T(8,128)S(1)} %get-tuple-element.257) | copy-start | bytes 2359300
  812.7 63.1 %copy-start.32 = (f32[1,768,256]{2,1,0:T(8,128)}, f32[1,768,256]{2,1,0:T(8,128)S(1)}, u32[]{:S(2)}) copy-start(f32[1,768,256]{2,1,0:T(8,128)S(1)} %get-tuple-element.259) | copy-start | bytes 2359300
  875.9 33.6 %reduce-scatter.46.cloned.1.call-start = ((), (), s32[]{:S(2)}) async-start(), calls=%async_computation.29 | async-start | bytes 1179648 | tf_op jit(solution)/shard_map/reduce_scatter | solution.py:144
  878.0 74.7 %reduce-scatter.48.cloned.1.call-start = ((), (), s32[]{:S(2)}) async-start(), calls=%async_computation.30 | async-start | bytes 1179648 | tf_op jit(solution)/shard_map/reduce_scatter | solution.py:144
  929.6 40.4 %reduce-scatter.40.cloned.1.call-start = ((), (), s32[]{:S(2)}) async-start(), calls=%async_computation.26 | async-start | bytes 1179648 | tf_op jit(solution)/shard_map/reduce_scatter | solution.py:144
  952.4 63.9 %reduce-scatter.50.cloned.1.call-start = ((), (), s32[]{:S(2)}) async-start(), calls=%async_computation.31 | async-start | bytes 1179648 | tf_op jit(solution)/shard_map/reduce_scatter | solution.py:152
  993.4 40.4 %reduce-scatter.58.cloned.1.call-start = ((), (), s32[]{:S(2)}) async-start(), calls=%async_computation.35 | async-start | bytes 1179648 | tf_op jit(solution)/shard_map/reduce_scatter | solution.py:152
  1016.2 118.6 %reduce-scatter.52.cloned.1.call-start = ((), (), s32[]{:S(2)}) async-start(), calls=%async_computation.32 | async-start | bytes 1179648 | tf_op jit(solution)/shard_map/reduce_scatter | solution.py:152
  1067.2 42.7 %copy-start.15 = (f32[2,768,256]{2,1,0:T(8,128)S(1)}, f32[2,768,256]{2,1,0:T(8,128)}, u32[]{:S(2)}) copy-start(f32[2,768,256]{2,1,0:T(8,128)} %copy-done.14) | copy-start | bytes 4718596
  1067.2 42.7 %copy-start.163 = (f32[256]{0:T(256)S(1)}, f32[256]{0:T(256)}, u32[]{:S(2)}) copy-start(f32[256]{0:T(256)} %copy-done.162) | copy-start | bytes 3076
  1067.2 42.6 %copy-start.165 = (f32[256]{0:T(256)S(1)}, f32[256]{0:T(256)}, u32[]{:S(2)}) copy-start(f32[256]{0:T(256)} %copy-done.164) | copy-start | bytes 3076
  1067.2 42.6 %copy-start.167 = (f32[256]{0:T(256)S(1)}, f32[256]{0:T(256)}, u32[]{:S(2)}) copy-start(f32[256]{0:T(256)} %copy-done.166) | copy-start | bytes 3076
  1067.2 42.6 %copy-start.169 = (f32[256]{0:T(256)S(1)}, f32[256]{0:T(256)}, u32[]{:S(2)}) copy-start(f32[256]{0:T(256)} %copy-done.168) | copy-start | bytes 3076
  1067.2 42.6 %copy-start.171 = (f32[256]{0:T(256)S(1)}, f32[256]{0:T(256)}, u32[]{:S(2)}) copy-start(f32[256]{0:T(256)} %copy-done.170) | copy-start | bytes 3076
  1067.2 42.6 %copy-start.173 = (f32[256]{0:T(256)S(1)}, f32[256]{0:T(256)}, u32[]{:S(2)}) copy-start(f32[256]{0:T(256)} %copy-done.172) | copy-start | bytes 3076
  1067.2 42.6 %copy-start.175 = (f32[256]{0:T(256)S(1)}, f32[256]{0:T(256)}, u32[]{:S(2)}) copy-start(f32[256]{0:T(256)} %copy-done.174) | copy-start | bytes 3076
  1067.2 42.6 %copy-start.177 = (f32[256]{0:T(256)S(1)}, f32[256]{0:T(256)}, u32[]{:S(2)}) copy-start(f32[256]{0:T(256)} %copy-done.176) | copy-start | bytes 3076
  1067.2 42.6 %copy-start.179 = (f32[256]{0:T(256)S(1)}, f32[256]{0:T(256)}, u32[]{:S(2)}) copy-start(f32[256]{0:T(256)} %copy-done.178) | copy-start | bytes 3076
  1067.2 42.6 %copy-start.181 = (f32[256]{0:T(256)S(1)}, f32[256]{0:T(256)}, u32[]{:S(2)}) copy-start(f32[256]{0:T(256)} %copy-done.180) | copy-start | bytes 3076
  1067.3 42.6 %copy-start.183 = (f32[256]{0:T(256)S(1)}, f32[256]{0:T(256)}, u32[]{:S(2)}) copy-start(f32[256]{0:T(256)} %copy-done.182) | copy-start | bytes 3076
  1067.3 42.6 %copy-start.185 = (f32[256]{0:T(256)S(1)}, f32[256]{0:T(256)}, u32[]{:S(2)}) copy-start(f32[256]{0:T(256)} %copy-done.184) | copy-start | bytes 3076
  1067.3 42.6 %copy-start.187 = (f32[256]{0:T(256)S(1)}, f32[256]{0:T(256)}, u32[]{:S(2)}) copy-start(f32[256]{0:T(256)} %copy-done.186) | copy-start | bytes 3076
  1067.3 42.6 %copy-start.189 = (f32[256]{0:T(256)S(1)}, f32[256]{0:T(256)}, u32[]{:S(2)}) copy-start(f32[256]{0:T(256)} %copy-done.188) | copy-start | bytes 3076
  1067.3 42.6 %copy-start.191 = (f32[256]{0:T(256)S(1)}, f32[256]{0:T(256)}, u32[]{:S(2)}) copy-start(f32[256]{0:T(256)} %copy-done.190) | copy-start | bytes 3076
  1067.3 42.6 %copy-start.193 = (f32[256]{0:T(256)S(1)}, f32[256]{0:T(256)}, u32[]{:S(2)}) copy-start(f32[256]{0:T(256)} %copy-done.192) | copy-start | bytes 3076
  1067.3 42.6 %copy-start.195 = (f32[256]{0:T(256)S(1)}, f32[256]{0:T(256)}, u32[]{:S(2)}) copy-start(f32[256]{0:T(256)} %copy-done.194) | copy-start | bytes 3076
  1117.8 34.2 %reduce-scatter.60.cloned.1.call-start = ((), (), s32[]{:S(2)}) async-start(), calls=%async_computation.36 | async-start | bytes 1179648 | tf_op jit(solution)/shard_map/reduce_scatter | solution.py:152
  1134.6 330.1 %reduce-scatter.54.cloned.1.call-start = ((), (), s32[]{:S(2)}) async-start(), calls=%async_computation.33 | async-start | bytes 1179648 | tf_op jit(solution)/shard_map/reduce_scatter | solution.py:152
  1333.9 143.6 %reduce-scatter.62.cloned.1.call-start = ((), (), s32[]{:S(2)}) async-start(), calls=%async_computation.37 | async-start | bytes 1179648 | tf_op jit(solution)/shard_map/reduce_scatter | solution.py:152
  1459.9 157.0 %reduce-scatter.56.cloned.1.call-start = ((), (), s32[]{:S(2)}) async-start(), calls=%async_computation.34 | async-start | bytes 1179648 | tf_op jit(solution)/shard_map/reduce_scatter | solution.py:152
  1499.9 117.0 %reduce-scatter.64.cloned.1.call-start = ((), (), s32[]{:S(2)}) async-start(), calls=%async_computation.38 | async-start | bytes 1179648 | tf_op jit(solution)/shard_map/reduce_scatter | solution.py:152
  1529.4 106.6 %reduce-scatter.72.cloned.1.call-start = ((), (), s32[]{:S(2)}) async-start(), calls=%async_computation.45 | async-start | bytes 69632
  1559.2 107.4 %reduce-scatter.70.cloned.1.call-start = ((), (), s32[]{:S(2)}) async-start(), calls=%async_computation.44 | async-start | bytes 69632
  1563.5 157.5 %reduce-scatter.74.cloned.1.call-start = ((), (), s32[]{:S(2)}) async-start(), calls=%async_computation.46 | async-start | bytes 69632
  1583.0 202.9 %reduce-scatter.68.cloned.1.call-start = ((), (), s32[]{:S(2)}) async-start(), calls=%async_computation.40 | async-start | bytes 2228224 | tf_op jit(solution)/shard_map/reduce_scatter | solution.py:507
  1591.4 301.2 %all-reduce.17.cloned.1.call-start = ((), (), s32[]{:S(2)}) async-start(), calls=%async_computation.49 | async-start | bytes 6291456
  1616.6 410.6 %reduce-scatter.78.cloned.1.call-start = ((), (), s32[]{:S(2)}) async-start(), calls=%async_computation.48 | async-start | bytes 270336
  1624.0 535.3 %reduce-scatter.76.cloned.1.call-start = ((), (), s32[]{:S(2)}) async-start(), calls=%async_computation.47 | async-start | bytes 270336
  1627.0 593.3 %reduce-scatter.66.cloned.1.call-start = ((), (), s32[]{:S(2)}) async-start(), calls=%async_computation.39 | async-start | bytes 2228224 | tf_op jit(solution)/shard_map/reduce_scatter | solution.py:501
  1632.7 267.1 %copy-start.59 = (f32[384,512]{1,0:T(8,128)S(1)}, f32[384,512]{1,0:T(8,128)}, u32[]{:S(2)}) copy-start(f32[384,512]{1,0:T(8,128)} %get-tuple-element.237) | copy-start | bytes 2359300
  1632.7 267.1 %copy-start.63 = (bf16[384,512]{1,0:T(8,128)(2,1)S(1)}, bf16[384,512]{1,0:T(8,128)(2,1)}, u32[]{:S(2)}) copy-start(bf16[384,512]{1,0:T(8,128)(2,1)} %reduce-scatter.56.cloned.1.call-done) | copy-start | bytes 1179652
  (266 other events, 3309.5 us)
Sparse Core Ops, SparseCore 0:
  10.2 43.9 all-gather.11
  56.4 40.5 all-gather.13
  186.2 15.1 reduce-scatter.33
  203.7 40.0 all-gather.15
  246.6 16.1 reduce-scatter.41
  508.6 14.8 reduce-scatter.35
  711.4 14.9 reduce-scatter.43
  876.0 13.6 reduce-scatter.37
  892.0 17.4 reduce-scatter.45
  929.7 20.0 reduce-scatter.47
  952.5 17.4 reduce-scatter.39
  993.5 20.2 reduce-scatter.49
  1016.4 17.4 reduce-scatter.57
  1117.9 13.7 reduce-scatter.51
  1134.8 17.1 reduce-scatter.59
  1334.0 17.4 reduce-scatter.53
  1460.0 17.4 reduce-scatter.61
  1500.0 24.9 reduce-scatter.55
  1529.5 17.4 reduce-scatter.63
  1559.3 51.9 reduce-scatter.71
  1615.7 50.9 reduce-scatter.69
  1670.0 50.9 reduce-scatter.73
  1725.2 60.6 reduce-scatter.67
  1789.5 102.9 all-reduce.16
  1894.8 132.3 reduce-scatter.77
  2029.9 129.3 reduce-scatter.75
  2162.8 57.4 reduce-scatter.65
where the time goes:
time: 2240 us; the launch traced here: 2230 us
  waiting for transfers between devices  668 us (30%)
  local copies, waits for them, and re-layouts  659 us (29%)
  blocking collectives  520 us (23%)
  matrix products  206 us (9%)
  other arithmetic  156 us (7%)
    unnamed x33, waiting for transfers between devices  444 us
    unnamed x664, local copies, waits for them, and re-layouts  324 us
    all_gather x8, blocking collectives, spread_grad(): return lax.all_gather(local_values, 'mp', axis=0, tiled=True)  102 us
    all_gather x8, blocking collectives, spread(): return lax.all_gather(local_values, 'mp', axis=0, tiled=True)  93.8 us
    all_gather x1, blocking collectives, per_device(): lax.all_gather(ln_bias, ('dp', 'mp'), axis=2, tiled=True)  71.6 us
    all_gather x1, blocking collectives, per_device(): lax.all_gather(ln_gain, ('dp', 'mp'), axis=2, tiled=True)  64.9 us
    reduce_scatter x1, waiting for transfers between devices, per_device(): lax.psum_scatter(stacked_grads[2].astype(jnp.bfloat16), 'dp', scatter_dim...  63.5 us
    reduce_scatter x1, waiting for transfers between devices, per_device(): lax.psum_scatter(stacked_grads[0].astype(jnp.bfloat16), 'dp', scatter_dim...  59.6 us
  transfers between devices with their start and end apart: 27, of which 14 were waited for; matrix products, arithmetic and copies ran while one was open for 25% of the time, Pallas kernels for 0%

commit v1 on v0

v1 whole, which is shorter than its diff:
```python
import math

import jax
import jax.numpy as jnp
from jax import lax
from jax.sharding import PartitionSpec as P

D = 512
HEADS = 8
HEAD_DIM = 64
FF = 2048
KERNEL = 31
LENGTH = 768
LANES = 128

epsilon = 1e-05
bfloat = jnp.bfloat16
single = jnp.float32
EVERY = ("mp", "dp")


def dot(spec, left, right):
    return jnp.einsum(spec, left, right, preferred_element_type=single)


def sinusoids(length, width):
    frequency = jnp.exp(
        jnp.arange(width // 2).astype(single) * (-2.0 * math.log(10000.0) / width)
    )
    angles = jnp.arange(length).astype(single)[:, None] * frequency[None, :]
    return (jnp.sin(angles), jnp.cos(angles))


def norm_rows(values, gain_row, bias_row):
    center = jnp.mean(values, axis=-1, keepdims=True)
    offset = values - center
    inverse_std = lax.rsqrt(jnp.mean(offset * offset, axis=-1, keepdims=True) + epsilon)
    unit_rows = offset * inverse_std
    return (unit_rows * gain_row + bias_row, (unit_rows, inverse_std))


def norm_rows_back(grad_normed, kept, gain_row):
    unit_rows, inverse_std = kept
    grad_unit = grad_normed * gain_row
    grad_values = inverse_std * (
        grad_unit
        - jnp.mean(grad_unit, axis=-1, keepdims=True)
        - unit_rows * jnp.mean(grad_unit * unit_rows, axis=-1, keepdims=True)
    )
    return (grad_values, jnp.sum(grad_normed * unit_rows, axis=0), jnp.sum(grad_normed, axis=0))


def swish_slope(values):
    sigmoid = jax.nn.sigmoid(values)
    return sigmoid * (1.0 + values * (1.0 - sigmoid))


def depthwise(gated, taps):
    kernel_size = taps.shape[0]
    margin = (kernel_size - 1) // 2
    length = gated.shape[1]
    padded = jnp.pad(gated, ((0, 0), (margin, margin), (0, 0)))
    convolved = jnp.zeros_like(gated)
    for tap_index in range(kernel_size):
        convolved = convolved + taps[tap_index] * padded[:, tap_index : tap_index + length, :]
    return convolved


def depthwise_back(gated, grad_convolved, taps):
    kernel_size = taps.shape[0]
    margin = (kernel_size - 1) // 2
    length = gated.shape[1]
    padded = jnp.pad(gated, ((0, 0), (margin, margin), (0, 0)))
    grad_padded = jnp.pad(grad_convolved, ((0, 0), (margin, margin), (0, 0)))
    grad_gated = jnp.zeros_like(gated)
    grad_taps = []
    for tap_index in range(kernel_size):
        begin = 2 * margin - tap_index
        grad_gated = grad_gated + taps[tap_index] * grad_padded[:, begin : begin + length, :]
        grad_taps.append(
            jnp.sum(padded[:, tap_index : tap_index + length, :] * grad_convolved, axis=(0, 1))
        )
    return (grad_gated, jnp.stack(grad_taps))


def per_device(
    inputs,
    ff_in,
    ff_out,
    in_mats,
    attn_out,
    conv_out,
    dw_kernel,
    bn_affine,
    pos_bias,
    ln_gain,
    ln_bias,
    cotangent,
):
    mp = lax.axis_size("mp")
    dp = lax.axis_size("dp")
    owners = mp * dp
    micro = inputs.shape[0]
    local_rows = inputs.shape[1]
    group_rows = local_rows * mp
    sequences = group_rows // LENGTH
    total_rows = group_rows * dp
    own = D // owners
    depth = D // dp
    score_scale = HEAD_DIM ** (-0.5)
    me = lax.axis_index("mp")
    mine = me % micro
    swap = [(0, 1), (1, 0)]
    paired = mp == 2 and micro == 2

    def enter(blocks):
        if paired:
            other = lax.ppermute(jnp.where(me == 0, blocks[1], blocks[0]), "mp", swap)
            first = jnp.where(me == 0, blocks[0], other)
            second = jnp.where(me == 0, other, blocks[1])
            return jnp.concatenate([first, second], axis=0)
        whole = lax.all_gather(blocks, "mp", axis=1, tiled=True)
        return lax.dynamic_index_in_dim(whole, mine, axis=0, keepdims=False)

    def leave(rows):
        if paired:
            upper, lower = rows[:local_rows], rows[local_rows:]
            sent = jnp.where(me == 0, lower, upper).astype(bfloat)
            other = lax.ppermute(sent, "mp", swap).astype(single)
            return jnp.stack(
                [jnp.where(me == 0, upper, other), jnp.where(me == 0, other, lower)]
            )
        whole = lax.all_gather(rows.astype(bfloat), "mp", axis=0)[:micro]
        return lax.dynamic_slice_in_dim(whole, me * local_rows, local_rows, axis=1).astype(single)

    pair_in = ff_in[0]
    pair_out = jnp.swapaxes(ff_out[0], 1, 2)
    gain_high = lax.reduce_precision(ln_gain[0], 8, 7)
    bias_high = lax.reduce_precision(ln_bias[0], 8, 7)
    small = jnp.concatenate(
        [
            dw_kernel[0],
            bn_affine[0],
            pos_bias[0],
            gain_high.astype(bfloat),
            bias_high.astype(bfloat),
            (ln_gain[0] - gain_high).astype(bfloat),
            (ln_bias[0] - bias_high).astype(bfloat),
        ],
        axis=0,
    )
    small_rows = small.shape[0]

    def fold(flat):
        spacing = [(0, 0)] * (flat.ndim - 1) + [(0, depth * LANES - flat.shape[-1])]
        return jnp.pad(flat, spacing).reshape(flat.shape[:-1] + (depth, LANES))

    def gather(parts):
        block = jnp.concatenate(parts, axis=1)
        return lax.all_gather(block, EVERY, axis=0, tiled=True).reshape(mp, D, -1)

    def unpack(packed, first, width):
        part = packed[:, :, first : first + width]
        return jnp.swapaxes(part, 0, 1).reshape(D, mp * width)

    hidden_width = FF // mp
    width = D // mp
    packed = gather([pair_in[0], pair_out[0], fold(small.reshape(-1))])
    in_zero = unpack(packed, 0, hidden_width)
    out_zero = unpack(packed, hidden_width, hidden_width)
    small_all = (
        packed[:, :, 2 * hidden_width :]
        .reshape(owners, depth * LANES)[:, : small_rows * own]
        .reshape(owners, small_rows, own)
    )
    channel_rows = KERNEL + 4
    channel = jnp.swapaxes(small_all[:, :channel_rows], 0, 1).reshape(channel_rows, D)
    channel = channel.astype(single)
    norm_rows_all = (
        small_all[:, channel_rows:]
        .reshape(mp, dp, 4, 5, own)
        .transpose(2, 3, 1, 0, 4)
        .reshape(4, 5, D)
        .astype(single)
    )
    norm_gain = norm_rows_all[0] + norm_rows_all[2]
    norm_bias = norm_rows_all[1] + norm_rows_all[3]
    taps, affine, biases = channel[:KERNEL], channel[KERNEL : KERNEL + 2], channel[KERNEL + 2 :]

    packed = gather(
        [in_mats[0, k] for k in range(6)] + [attn_out[0].T, conv_out[0].T]
    )
    mats = [unpack(packed, k * width, width) for k in range(8)]
    w_position, w_attn, w_conv = (mats[3], mats[6], mats[7])
    w_query = jnp.concatenate(mats[0:3], axis=1)
    w_gate = jnp.concatenate(mats[4:6], axis=1)
    packed = gather([pair_in[1], pair_out[1]])
    in_one = unpack(packed, 0, hidden_width)
    out_one = unpack(packed, hidden_width, hidden_width)

    def norm_input(values, slot):
        normed, kept = norm_rows(values, norm_gain[slot], norm_bias[slot])
        return (normed.astype(bfloat), kept)

    def ff_forward(rows, w_first, w_second):
        hidden_pre = dot("gd,df->gf", rows, w_first)
        hidden = jax.nn.silu(hidden_pre).astype(bfloat)
        return (dot("gf,df->gd", hidden, w_second), (hidden_pre, hidden))

    def ff_backward(grad_out, rows, kept, w_first, w_second):
        hidden_pre, hidden = kept
        grad_second = dot("gd,gf->df", grad_out, hidden)
        grad_hidden = dot("gd,df->gf", grad_out, w_second)
        grad_pre = (grad_hidden * swish_slope(hidden_pre)).astype(bfloat)
        grad_first = dot("gd,gf->df", rows, grad_pre)
        return (dot("gf,df->gd", grad_pre, w_first), grad_first, grad_second)

    sine, cosine = sinusoids(LENGTH, D)
    angle_rows = jnp.concatenate([cosine, sine], axis=1).astype(bfloat)
    position_heads = w_position.reshape(D, HEADS, HEAD_DIM)

    def by_head(values):
        return values.reshape(sequences, LENGTH, HEADS, HEAD_DIM).transpose(0, 2, 1, 3)

    def by_row(values):
        return values.transpose(0, 2, 1, 3).reshape(group_rows, D)

    def attention_forward(rows):
        projected = dot("gd,dc->gc", rows, w_query)
        query_rows = projected[:, :D]
        key_rows = by_head(projected[:, D : 2 * D].astype(bfloat))
        value_rows = by_head(projected[:, 2 * D :].astype(bfloat))
        with_content = by_head((score_scale * (query_rows + biases[0])).astype(bfloat))
        with_position = by_head((score_scale * (query_rows + biases[1])).astype(bfloat))
        turned = dot("shid,khd->shik", with_position, position_heads)
        on_sine, on_cosine = turned[..., : D // 2], turned[..., D // 2 :]
        turned = jnp.concatenate(
            [on_sine * sine + on_cosine * cosine, on_cosine * sine - on_sine * cosine], axis=-1
        ).astype(bfloat)
        scores = dot("shid,shjd->shij", with_content, key_rows) + dot(
            "shik,jk->shij", turned, angle_rows
        )
        row_max = jnp.max(scores, axis=-1, keepdims=True)
        exponent = jnp.exp(scores - row_max)
        row_total = jnp.sum(exponent, axis=-1, keepdims=True)
        probs = (exponent / row_total).astype(bfloat)
        context = dot("shij,shjd->shid", probs, value_rows)
        context_rows = by_row(context.astype(bfloat))
        branch = dot("gc,dc->gd", context_rows, w_attn)
        return (
            branch,
            (with_content, with_position, key_rows, value_rows, probs, context, context_rows),
        )

    def attention_backward(grad_out, rows, kept):
        with_content, with_position, key_rows, value_rows, probs, context, context_rows = kept
        grad_attn = dot("gd,gc->dc", grad_out, context_rows)
        grad_context = by_head(dot("gd,dc->gc", grad_out, w_attn).astype(bfloat))
        grad_probs = dot("shid,shjd->shij", grad_context, value_rows)
        grad_value = dot("shij,shid->shjd", probs, grad_context)
        shared = jnp.sum(grad_context.astype(single) * context, axis=-1, keepdims=True)
        grad_scores = (probs.astype(single) * (grad_probs - shared)).astype(bfloat)
        grad_content = dot("shij,shjd->shid", grad_scores, key_rows)
        grad_key = dot("shij,shid->shjd", grad_scores, with_content)
        grad_turned = dot("shij,jk->shik", grad_scores, angle_rows)
        on_first, on_second = grad_turned[..., : D // 2], grad_turned[..., D // 2 :]
        grad_turned = jnp.concatenate(
            [on_first * sine - on_second * cosine, on_first * cosine + on_second * sine], axis=-1
        ).astype(bfloat)
        grad_posq = dot("shik,khd->shid", grad_turned, position_heads)
        grad_position = dot("shik,shid->khd", grad_turned, with_position).reshape(D, D)
        grad_bias = score_scale * jnp.stack(
            [
                jnp.sum(grad_content, axis=(0, 2)).reshape(D),
                jnp.sum(grad_posq, axis=(0, 2)).reshape(D),
            ]
        )
        stacked = jnp.concatenate(
            [
                by_row((score_scale * (grad_content + grad_posq)).astype(bfloat)),
                by_row(grad_key.astype(bfloat)),
                by_row(grad_value.astype(bfloat)),
            ],
            axis=1,
        )
        grad_query = dot("gd,gc->dc", rows, stacked)
        grad_rows = dot("gc,dc->gd", stacked, w_query)
        return (grad_rows, grad_query, grad_position, grad_attn, grad_bias)

    values = enter(inputs).astype(single)
    cotangent_rows = enter(cotangent).astype(single)
    rows_one, norm_one = norm_input(values, 0)
    branch, ff_first = ff_forward(rows_one, in_zero, out_zero)
    after_one = values + 0.5 * branch
    rows_two, norm_two = norm_input(after_one, 1)
    branch, attn_kept = attention_forward(rows_two)
    after_two = after_one + branch
    rows_three, norm_three = norm_input(after_two, 2)
    projected = dot("gd,dc->gc", rows_three, w_gate)
    linear_part, gate_part = projected[:, :D], projected[:, D:]
    gated = (linear_part * jax.nn.sigmoid(gate_part)).reshape(sequences, LENGTH, D)
    convolved = depthwise(gated, taps).reshape(group_rows, D)
    local_center = jnp.mean(convolved, axis=0)
    local_offset = convolved - local_center
    moments = lax.all_gather(
        jnp.stack([local_center, jnp.sum(local_offset * local_offset, axis=0)]), "dp", axis=0
    )
    center = jnp.mean(moments[:, 0], axis=0)
    spread = moments[:, 0] - center
    variance = (jnp.sum(moments[:, 1], axis=0) + group_rows * jnp.sum(spread * spread, axis=0)) / (
        total_rows
    )
    inverse_std = lax.rsqrt(variance + epsilon)
    unit_values = (convolved - center) * inverse_std
    scaled = unit_values * affine[0] + affine[1]
    active = jax.nn.silu(scaled).astype(bfloat)
    after_three = after_two + dot("gc,dc->gd", active, w_conv)
    rows_four, norm_four = norm_input(after_three, 3)
    branch, ff_second = ff_forward(rows_four, in_one, out_one)
    after_four = after_three + 0.5 * branch
    result, norm_five = norm_rows(after_four, norm_gain[4], norm_bias[4])
    outputs = leave(result)

    counts = (me < micro).astype(single)

    def scatter(parts):
        blocks = [
            jnp.swapaxes(part.astype(bfloat).reshape(D, mp, -1), 0, 1) for part in parts[0]
        ] + parts[1]
        block = jnp.concatenate(blocks, axis=2)
        if mp != micro:
            block = block * counts.astype(bfloat)
        return lax.psum_scatter(
            block.reshape(mp * D, -1), EVERY, scatter_dimension=0, tiled=True
        ).astype(single)

    gains = [None] * 5
    shifts = [None] * 5
    grad_four, gains[4], shifts[4] = norm_rows_back(cotangent_rows, norm_five, norm_gain[4])
    grad_rows, first_one, second_one = ff_backward(
        (0.5 * grad_four).astype(bfloat), rows_four, ff_second, in_one, out_one
    )
    owned_one = scatter(([first_one, second_one], []))
    grad_norm, gains[3], shifts[3] = norm_rows_back(grad_rows, norm_four, norm_gain[3])
    grad_three = grad_four + grad_norm
    grad_out = grad_three.astype(bfloat)
    grad_conv = dot("gd,gc->dc", grad_out, active)
    grad_scaled = dot("gd,dc->gc", grad_out, w_conv) * swish_slope(scaled)
    local_shift = jnp.sum(grad_scaled, axis=0)
    local_scale = jnp.sum(grad_scaled * unit_values, axis=0)
    sums = jnp.sum(lax.all_gather(jnp.stack([local_shift, local_scale]), "dp", axis=0), axis=0)
    grad_convolved = (
        affine[0]
        * inverse_std
        * (grad_scaled - sums[0] / total_rows - unit_values * (sums[1] / total_rows))
    )
    grad_gated, grad_taps = depthwise_back(
        gated, grad_convolved.reshape(sequences, LENGTH, D), taps
    )
    grad_gated = grad_gated.reshape(group_rows, D)
    sigmoid = jax.nn.sigmoid(gate_part)
    stacked = jnp.concatenate(
        [
            (grad_gated * sigmoid).astype(bfloat),
            (grad_gated * linear_part * sigmoid * (1.0 - sigmoid)).astype(bfloat),
        ],
        axis=1,
    )
    grad_gate = dot("gd,gc->dc", rows_three, stacked)
    grad_rows = dot("gc,dc->gd", stacked, w_gate)
    grad_norm, gains[2], shifts[2] = norm_rows_back(grad_rows, norm_three, norm_gain[2])
    grad_two = grad_three + grad_norm
    grad_rows, grad_query, grad_position, grad_attn, grad_bias = attention_backward(
        grad_two.astype(bfloat), rows_two, attn_kept
    )
    owned_mats = scatter(
        (
            [grad_query[:, k * D : (k + 1) * D] for k in range(3)]
            + [grad_position, grad_gate[:, :D], grad_gate[:, D:], grad_attn, grad_conv],
            [],
        )
    )
    grad_norm, gains[1], shifts[1] = norm_rows_back(grad_rows, norm_two, norm_gain[1])
    grad_one = grad_two + grad_norm
    grad_rows, first_zero, second_zero = ff_backward(
        (0.5 * grad_one).astype(bfloat), rows_one, ff_first, in_zero, out_zero
    )
    grad_norm, gains[0], shifts[0] = norm_rows_back(grad_rows, norm_one, norm_gain[0])
    input_grad = leave(grad_one + grad_norm)
    channel_grads = jnp.concatenate(
        [grad_taps, jnp.stack([local_scale, local_shift]), grad_bias], axis=0
    )
    channel_grads = jnp.swapaxes(channel_grads.reshape(channel_rows, owners, own), 0, 1)
    norm_grads = (
        jnp.stack(gains + shifts).reshape(10, dp, mp, own).transpose(2, 1, 0, 3)
    ).reshape(owners, 10, own)
    small_grads = jnp.concatenate([channel_grads, norm_grads], axis=1).reshape(owners, -1)
    owned_zero = scatter(
        ([first_zero, second_zero], [fold(small_grads.astype(bfloat)).reshape(mp, D, LANES)])
    )
    owned_small = owned_zero[:, 2 * hidden_width :].reshape(-1)[: (channel_rows + 10) * own]
    owned_small = owned_small.reshape(1, channel_rows + 10, own)

    def halves(owned):
        return (owned[:, :hidden_width], owned[:, hidden_width : 2 * hidden_width].T)

    first_zero, second_zero = halves(owned_zero)
    first_one, second_one = halves(owned_one)
    owned_list = [owned_mats[:, k * width : (k + 1) * width] for k in range(8)]
    return (
        outputs,
        input_grad,
        jnp.stack([first_zero, first_one])[None],
        jnp.stack([second_zero, second_one])[None],
        jnp.stack(owned_list[:6])[None],
        owned_list[6].T[None],
        owned_list[7].T[None],
        owned_small[:, :KERNEL],
        owned_small[:, KERNEL : KERNEL + 2],
        owned_small[:, KERNEL + 2 : channel_rows],
        owned_small[:, channel_rows : channel_rows + 5],
        owned_small[:, channel_rows + 5 :],
    )


def solution(mesh):
    placed = (
        P(None, ("dp", "mp"), None),
        P(None, None, "dp", "mp"),
        P(None, None, "mp", "dp"),
        P(None, None, "dp", "mp"),
        P(None, "mp", "dp"),
        P(None, "mp", "dp"),
        P(None, None, ("mp", "dp")),
        P(None, None, ("mp", "dp")),
        P(None, None, ("mp", "dp")),
        P(None, None, ("dp", "mp")),
        P(None, None, ("dp", "mp")),
        P(None, ("dp", "mp"), None),
    )
    return jax.shard_map(
        per_device,
        mesh=mesh,
        in_specs=placed,
        out_specs=(
            P(None, ("dp", "mp"), None),
            P(None, ("dp", "mp"), None),
            P(None, None, "dp", "mp"),
            P(None, None, "mp", "dp"),
            P(None, None, "dp", "mp"),
            P(None, "mp", "dp"),
            P(None, "mp", "dp"),
            P(None, None, ("mp", "dp")),
            P(None, None, ("mp", "dp")),
            P(None, None, ("mp", "dp")),
            P(None, None, ("dp", "mp")),
            P(None, None, ("dp", "mp")),
        ),
        check_vma=False,
    )
```

time: 2240 us -> 900 us (0.40)
  blocking collectives: 520 us -> 37.7 us
  local copies, waits for them, and re-layouts: 659 us -> 251 us
  waiting for transfers between devices: 668 us -> 338 us
  matrix products: 206 us -> 141 us
  other arithmetic: 156 us -> 95.9 us
    unnamed x33 -> x6, waiting for transfers between devices: 444 us -> 0.1 us
    all_gather x23 -> x2, blocking collectives: 429 us -> 37.7 us  [the longest x1 20.1 us: per_device(): lax.all_gather(jnp.stack([local_center, jnp.sum(local_offset * local_offs...]
    unnamed x664 -> x476, local copies, waits for them, and re-layouts: 324 us -> 32.2 us
    all_gather x3, waiting for transfers between devices: 0.01 us -> 133 us  [gather(): return lax.all_gather(block, EVERY, axis=0, tiled=True).reshape(mp, D, -1)]
    psum x3 -> x0, blocking collectives: 90.9 us -> none  [the longest x1 31.9 us: conv_backward(): sum_shift, sum_scale = lax.psum((local_shift, local_scale), 'dp')]
    reshape x6 -> x17, local copies, waits for them, and re-layouts: 112 us -> 33.1 us  [the longest x11 31.9 us: scatter(): part.astype(bfloat).reshape(D, mp, -1)]
    dot_general x69 -> x34, matrix products: 206 us -> 127 us  [dot(): return jnp.einsum(spec, left, right, preferred_element_type=single)]
    slice x12 -> x22, local copies, waits for them, and re-layouts: 85.3 us -> 10.4 us  [the longest x1 2.26 us: per_device(): grad_gate[:, D:]]
  transfers between devices with their start and end apart: 27 -> 10, of which waited for: 14 -> 9; matrix products, arithmetic and copies ran while one was open for 25% -> 30% of each run, Pallas kernels for 0% -> 0%
where the time goes in v1:
time: 900 us; the launch traced here: 888 us
  waiting for transfers between devices  338 us (38%)
  local copies, waits for them, and re-layouts  251 us (28%)
  matrix products  141 us (16%)
  other arithmetic  95.9 us (11%)
  blocking collectives  37.7 us (4%)
  between operations  17.6 us (2%)
    reduce_scatter x3, waiting for transfers between devices, scatter(): lax.psum_scatter(block.reshape(mp * D, -1), EVERY, scatter_dimension=0, t...  176 us
    all_gather x3, waiting for transfers between devices, gather(): return lax.all_gather(block, EVERY, axis=0, tiled=True).reshape(mp, D, -1)  133 us
    dot_general x34, matrix products, dot(): return jnp.einsum(spec, left, right, preferred_element_type=single)  127 us
    concatenate x34, local copies, waits for them, and re-layouts, per_device(): jnp.concatenate([grad_taps, jnp.stack([local_scale, local_shift]), grad_b...  54.5 us
    transpose x15, local copies, waits for them, and re-layouts, unpack(): return jnp.swapaxes(part, 0, 1).reshape(D, mp * width)  40.4 us
    unnamed x476, local copies, waits for them, and re-layouts  32.2 us
    reshape x11, local copies, waits for them, and re-layouts, scatter(): part.astype(bfloat).reshape(D, mp, -1)  31.9 us
    mul x31, local copies, waits for them, and re-layouts, depthwise(): taps[tap_index] * padded[:, tap_index:tap_index + length, :]  20.1 us
  transfers between devices with their start and end apart: 10, of which 9 were waited for; matrix products, arithmetic and copies ran while one was open for 30% of the time, Pallas kernels for 0%

profile of v1, /device:TPU:0, one launch (start us, length us, event | category | flops | bytes accessed | tf_op | source)
XLA Modules:
  0.0 887.5 jit_solution(970487730865054116)
XLA Ops:
  26.9 3.8 fusion.95
  33.1 3.6 collective-permute-done
  37.2 7.6 collective-permute-done.2
  47.4 31.9 %all-gather.10.cloned.1.call-done = bf16[1024,2048]{1,0:T(8,128)(2,1)} async-done(((bf16[32,2048]{1,0:T(8,128)(2,1)}), bf16[1024,2048]{1,0:T(8,128)(2,1)}) %all-gather.10.cloned.1.call-update) | async-done | bytes 4194320 | tf_op jit(solution)/shard_map/all_gather | solution.py:160
  79.3 3.7 slice_bitcast_fusion.6
  85.0 58.3 %all-gather.12.cloned.1.call-done = bf16[1024,2048]{1,0:T(8,128)(2,1)} async-done(((bf16[32,2048]{1,0:T(8,128)(2,1)}), bf16[1024,2048]{1,0:T(8,128)(2,1)}) %all-gather.12.cloned.1.call-update) | async-done | bytes 4194320 | tf_op jit(solution)/shard_map/all_gather | solution.py:160
  143.3 4.7 slice_bitcast_fusion
  148.0 3.9 copy.731
  161.5 3.9 copy.730
  165.4 42.9 %all-gather.8.cloned.1.call-done = bf16[1024,2176]{1,0:T(8,128)(2,1)} async-done(((bf16[32,2176]{1,0:T(8,128)(2,1)}), bf16[1024,2176]{1,0:T(8,128)(2,1)}) %all-gather.8.cloned.1.call-update) | async-done | bytes 4456464 | tf_op jit(solution)/shard_map/all_gather | solution.py:160
  209.4 4.7 slice_bitcast_fusion.2
  215.8 4.0 copy.678
  246.5 3.9 copy.677
  250.5 6.7 multiply_convert_fusion.4
  261.0 3.8 fusion.142
  267.8 3.1 multiply_convert_fusion.10
  275.5 3.2 convolution_bitcast_fusion
  280.8 9.3 %fusion.1 = f32[8,768,768]{1,2,0:T(8,128)} fusion(bf16[8,768,256]{1,2,0:T(8,128)(2,1)S(1)} %get-tuple-element.157, bf16[8,768,256]{1,2,0:T(8,128)(2,1)S(1)} %get-tuple-element.156, bf16[768,256]{1,0:T(8,128)(2,1)S(1)} %copy-done.81, bf16[768,256]{1,0:T(8,128)(2,1)S(1)} %copy-done.79), kind=kOutput, calls=%fused_computation.5 | convolution fusion | flops 4845993984 | bytes 25952256 | tf_op jit(solution)/shard_map/shik,jk->shij/dot_general | solution.py:23
  290.1 14.1 %fusion.143 = (f32[8,768]{1,0:T(8,128)}, f32[8,768,768]{1,2,0:T(8,128)}) fusion(f32[8,768,768]{1,2,0:T(8,128)} %fusion.1, bf16[8,768,64]{1,2,0:T(8,128)(2,1)} %bitcast.495, bf16[8,768,64]{1,2,0:T(8,128)(2,1)S(1)} %bitcast.489), kind=kOutput, calls=%fused_computation.385 | convolution fusion | flops 618136320 | bytes 39346176 | tf_op jit(solution)/shard_map/sub | solution.py:244
  304.1 7.2 divide_convert_fusion
  311.4 3.4 fusion.144
  321.4 6.5 fusion.128
  328.2 20.1 %all-gather.2 = f32[16,2,512]{2,1,0:T(2,128)S(1)} all-gather(f32[1,2,512]{2,1,0:T(2,128)S(1)} %maximum_bitcast_fusion.5), channel_id=2, replica_groups=mesh['dp'=16,'mp'=2] {'dp'}, dimensions={0}, use_global_device_ids=true | all-gather | bytes 69632 | tf_op jit(solution)/shard_map/all_gather | solution.py:305
  350.4 3.1 multiply_convert_fusion.3
  358.0 3.4 convolution_convert_fusion.1
  361.4 4.0 multiply_convert_fusion.2
  365.4 3.5 fusion.151
  368.9 3.2 convolution_convert_fusion.2
  372.1 3.0 copy.734
  375.2 3.2 multiply_reduce_fusion
  378.5 3.7 multiply_add_fusion.3
  386.8 17.6 %all-gather.3 = f32[16,2,512]{2,1,0:T(2,128)S(1)} all-gather(f32[1,2,512]{2,1,0:T(2,128)S(1)} %maximum_bitcast_fusion.6), channel_id=3, replica_groups=mesh['dp'=16,'mp'=2] {'dp'}, dimensions={0}, use_global_device_ids=true | all-gather | bytes 69632 | tf_op jit(solution)/shard_map/all_gather | solution.py:351
  404.8 3.5 multiply_reduce_fusion.6
  408.6 6.9 fusion.38
  421.7 3.0 copy.736
  424.8 3.2 multiply_reduce_fusion.1
  432.9 4.5 reshape.894
  437.4 4.5 reshape.895
  441.9 8.0 pad_maximum_fusion.2
  449.9 6.0 copy.792
  468.3 6.9 multiply_convert_fusion
  475.2 7.0 convolution_bitcast_fusion.1
  482.2 3.1 fusion.9
  485.3 5.8 fusion.76
  493.1 5.9 fusion.152
  499.1 4.9 bitcast_reduce_fusion
  504.1 3.8 convolution_convert_fusion.7
  508.0 6.8 convolution_convert_fusion.8
  530.0 3.9 copy.797
  600.4 4.3 fusion.149
  613.0 5.2 multiply_convert_fusion.1
  619.9 3.2 convolution_convert_fusion.4
  623.1 4.5 reshape.891
  627.6 3.6 copy.746
  631.3 5.1 convolution_convert_fusion.3
  636.3 4.5 reshape.892
  640.8 3.7 copy.747
  644.5 4.9 fusion.148
  657.8 5.2 concatenate.203
  664.6 4.1 pad_maximum_fusion.1
  674.5 10.2 %collective-permute-done.1 = bf16[384,512]{0,1:T(8,128)(2,1)S(1)} collective-permute-done((bf16[384,512]{0,1:T(8,128)(2,1)S(1)}, bf16[384,512]{0,1:T(8,128)(2,1)S(1)}, u32[]{:S(2)}, u32[]{:S(2)}) %collective-permute-start.1) | collective-permute-done | bytes 393248 | tf_op jit(solution)/shard_map/ppermute | solution.py:129
  686.5 7.6 collective-permute-done.3
  697.9 37.0 %reduce-scatter.8.cloned.1.call-done = bf16[32,2048]{1,0:T(8,128)(2,1)} async-done(((bf16[1024,2048]{1,0:T(8,128)(2,1)}), bf16[32,2048]{1,0:T(8,128)(2,1)}) %reduce-scatter.8.cloned.1.call-update) | async-done | bytes 131088 | tf_op jit(solution)/shard_map/reduce_scatter | solution.py:333
  736.6 138.9 %reduce-scatter.4.cloned.1.call-done = bf16[32,2176]{1,0:T(8,128)(2,1)} async-done(((bf16[1024,2176]{1,0:T(8,128)(2,1)}), bf16[32,2176]{1,0:T(8,128)(2,1)}) %reduce-scatter.4.cloned.1.call-update) | async-done | bytes 139280 | tf_op jit(solution)/shard_map/reduce_scatter | solution.py:333
  (774 shorter events, 241.2 us)
Async XLA Ops:
  7.2 14.1 %copy-start.62 = (bf16[2,384,512]{2,1,0:T(8,128)(2,1)S(1)}, bf16[2,384,512]{2,1,0:T(8,128)(2,1)}, u32[]{:S(2)}) copy-start(bf16[2,384,512]{2,1,0:T(8,128)(2,1)} %param.12) | copy-start | bytes 2359300
  7.2 72.1 %all-gather.10.cloned.1.call-start = ((), (), s32[]{:S(2)}) async-start(), calls=%async_computation.4 | async-start | bytes 4325376 | tf_op jit(solution)/shard_map/all_gather | solution.py:160
  13.7 129.6 %all-gather.12.cloned.1.call-start = ((), (), s32[]{:S(2)}) async-start(), calls=%async_computation.5 | async-start | bytes 4325376 | tf_op jit(solution)/shard_map/all_gather | solution.py:160
  16.2 192.1 %all-gather.8.cloned.1.call-start = ((), (), s32[]{:S(2)}) async-start(), calls=%async_computation.3 | async-start | bytes 4595712 | tf_op jit(solution)/shard_map/all_gather | solution.py:160
  21.3 675.7 %reduce-scatter.6.cloned.1.call-start = ((), (), s32[]{:S(2)}) async-start(), calls=%async_computation.7 | async-start | bytes 4325376 | tf_op jit(solution)/shard_map/reduce_scatter | solution.py:333
  22.6 14.1 %collective-permute-start = (bf16[384,512]{0,1:T(8,128)(2,1)}, bf16[384,512]{0,1:T(8,128)(2,1)S(1)}, u32[]{:S(2)}, u32[]{:S(2)}) collective-permute-start(bf16[384,512]{0,1:T(8,128)(2,1)} %bitcast_select_fusion.4), channel_id=1, source_target_pairs={{0,1},{1,0},{2,3},{3,2},{4,5},{5,4},{6,7},{7,6},{8,9},{9,8},{10,11... | collective-permute-start | bytes 1179656 | tf_op jit(solution)/shard_map/ppermute | solution.py:118
  26.9 17.9 %collective-permute-start.2 = (bf16[384,512]{0,1:T(8,128)(2,1)}, bf16[384,512]{0,1:T(8,128)(2,1)}, u32[]{:S(2)}, u32[]{:S(2)}) collective-permute-start(bf16[384,512]{0,1:T(8,128)(2,1)} %bitcast_select_fusion.1), channel_id=1, source_target_pairs={{0,1},{1,0},{2,3},{3,2},{4,5},{5,4},{6,7},{7,6},{8,9},{9,8},{10,11... | collective-permute-start | bytes 1179656 | tf_op jit(solution)/shard_map/ppermute | solution.py:118
  36.8 220.5 %copy-start.19 = (bf16[384,512]{0,1:T(8,128)(2,1)}, bf16[384,512]{0,1:T(8,128)(2,1)S(1)}, u32[]{:S(2)}) copy-start(bf16[384,512]{0,1:T(8,128)(2,1)S(1)} %get-tuple-element.195) | copy-start | bytes 1179652
  36.8 220.5 %copy-start.21 = (bf16[384,512]{0,1:T(8,128)(2,1)}, bf16[384,512]{0,1:T(8,128)(2,1)S(1)}, u32[]{:S(2)}) copy-start(bf16[384,512]{0,1:T(8,128)(2,1)S(1)} %get-tuple-element.196) | copy-start | bytes 1179652
  36.9 213.5 %copy-start.87 = (f32[768]{0:T(1024)}, f32[768]{0:T(1024)S(1)}, u32[]{:S(2)}) copy-start(f32[768]{0:T(1024)S(1)} %broadcast_multiply_fusion.14) | copy-start | bytes 9220
  37.2 213.3 %copy-start.91 = (f32[768]{0:T(1024)}, f32[768]{0:T(1024)S(1)}, u32[]{:S(2)}) copy-start(f32[768]{0:T(1024)S(1)} %add_rsqrt_fusion.4) | copy-start | bytes 9220
  159.5 100.0 %copy-start.45 = (bf16[512,2,256]{0,2,1:T(8,128)(2,1)}, bf16[512,2,256]{0,2,1:T(8,128)(2,1)S(1)}, u32[]{:S(2)}) copy-start(bf16[512,2,256]{0,2,1:T(8,128)(2,1)S(1)} %copy.681) | copy-start | bytes 1572868
  220.0 100.2 %copy-start.107 = (f32[512]{0:T(512)}, f32[512]{0:T(512)S(1)}, u32[]{:S(2)}) copy-start(f32[512]{0:T(512)S(1)} %mul.1192) | copy-start | bytes 6148
  245.7 13.8 %copy-start.89 = (f32[1,1,512]{2,0,1:T(1,128)}, f32[1,1,512]{2,0,1:T(1,128)S(1)}, u32[]{:S(2)}) copy-start(f32[1,1,512]{2,0,1:T(1,128)S(1)} %get-tuple-element.252) | copy-start | bytes 6148
  246.5 13.0 %copy-start.123 = (f32[1,1,512]{2,0,1:T(1,128)}, f32[1,1,512]{2,0,1:T(1,128)S(1)}, u32[]{:S(2)}) copy-start(f32[1,1,512]{2,0,1:T(1,128)S(1)} %get-tuple-element.257) | copy-start | bytes 6148
  250.5 6.8 copy-start.51
  259.2 56.3 %copy-start.2 = (f32[768,512]{0,1:T(8,128)}, f32[768,512]{0,1:T(8,128)S(1)}, u32[]{:S(2)}) copy-start(f32[768,512]{0,1:T(8,128)S(1)} %get-tuple-element.272) | copy-start | bytes 4718596
  266.1 24.0 %copy-start.26 = (bf16[768,512]{0,1:T(8,128)(2,1)}, bf16[768,512]{0,1:T(8,128)(2,1)S(1)}, u32[]{:S(2)}) copy-start(bf16[768,512]{0,1:T(8,128)(2,1)S(1)} %copy.684) | copy-start | bytes 2359300
  267.8 43.6 %copy-start.27 = (bf16[768,512]{0,1:T(8,128)(2,1)}, bf16[768,512]{0,1:T(8,128)(2,1)S(1)}, u32[]{:S(2)}) copy-start(bf16[768,512]{0,1:T(8,128)(2,1)S(1)} %copy.691) | copy-start | bytes 2359300
  316.4 32.1 %copy-start.7 = (f32[768,512]{0,1:T(8,128)}, f32[768,512]{0,1:T(8,128)S(1)}, u32[]{:S(2)}) copy-start(f32[768,512]{0,1:T(8,128)S(1)} %get-tuple-element.280) | copy-start | bytes 4718596
  327.9 55.9 %copy-start.13 = (f32[1,768,512]{2,1,0:T(8,128)}, f32[1,768,512]{2,1,0:T(8,128)S(1)}, u32[]{:S(2)}) copy-start(f32[1,768,512]{2,1,0:T(8,128)S(1)} %get-tuple-element.153) | copy-start | bytes 4718596
  327.9 20.6 %copy-start.77 = (bf16[512,2,256]{0,2,1:T(8,128)(2,1)S(1)}, bf16[512,2,256]{0,2,1:T(8,128)(2,1)}, u32[]{:S(2)}) copy-start(bf16[512,2,256]{0,2,1:T(8,128)(2,1)} %copy.729) | copy-start | bytes 1572868
  327.9 20.6 %copy-start.205 = (f32[512]{0:T(512)S(1)}, f32[512]{0:T(512)}, u32[]{:S(2)}) copy-start(f32[512]{0:T(512)} %mul.1298) | copy-start | bytes 6148
  327.9 20.6 %copy-start.207 = (f32[512]{0:T(512)S(1)}, f32[512]{0:T(512)}, u32[]{:S(2)}) copy-start(f32[512]{0:T(512)} %add.492) | copy-start | bytes 6148
  349.5 19.4 %copy-start.14 = (f32[768,512]{0,1:T(8,128)}, f32[768,512]{0,1:T(8,128)S(1)}, u32[]{:S(2)}) copy-start(f32[768,512]{0,1:T(8,128)S(1)} %get-tuple-element.282) | copy-start | bytes 4718596
  355.5 5.9 copy-start.16
  383.8 20.6 %copy-start.179 = (f32[512]{0:T(512)S(1)}, f32[512]{0:T(512)}, u32[]{:S(2)}) copy-start(f32[512]{0:T(512)} %copy-done.177) | copy-start | bytes 6148
  383.8 20.6 %copy-start.192 = (f32[1,512]{1,0:T(1,128)S(1)}, f32[1,512]{1,0:T(1,128)}, u32[]{:S(2)}) copy-start(f32[1,512]{1,0:T(1,128)} %slice.833) | copy-start | bytes 6148
  383.9 20.6 %copy-start.182 = (f32[512]{0:T(512)S(1)}, f32[512]{0:T(512)}, u32[]{:S(2)}) copy-start(f32[512]{0:T(512)} %copy-done.180) | copy-start | bytes 6148
  456.0 278.9 %reduce-scatter.8.cloned.1.call-start = ((), (), s32[]{:S(2)}) async-start(), calls=%async_computation.8 | async-start | bytes 4325376 | tf_op jit(solution)/shard_map/reduce_scatter | solution.py:333
  468.2 6.9 copy-start.80
  475.2 7.0 copy-start.1
  475.2 7.0 copy-start.31
  475.2 7.0 copy-start.33
  493.1 6.0 copy-start.42
  493.1 6.0 copy-start.43
  493.1 10.9 %slice-start = ((s8[9437184]{0:T(1024)(128)(4,1)}), s8[4194304]{0:T(1024)(128)(4,1)S(1)}, s32[]{:S(2)}) async-start(s8[9437184]{0:T(1024)(128)(4,1)} %bitcast.475), calls=%async_computation.9 | async-start | bytes 8388608
  493.1 10.9 %slice-start.1 = ((s8[9437184]{0:T(1024)(128)(4,1)}), s8[4194304]{0:T(1024)(128)(4,1)S(1)}, s32[]{:S(2)}) async-start(s8[9437184]{0:T(1024)(128)(4,1)} %bitcast.475), calls=%async_computation.10 | async-start | bytes 8388608
  507.9 6.9 copy-start.3
  507.9 6.9 copy-start.64
  507.9 6.9 copy-start.83
  507.9 6.9 copy-start.85
  507.9 6.9 copy-start.90
  507.9 6.9 copy-start.124
  507.9 6.9 copy-start.213
  533.9 341.6 %reduce-scatter.4.cloned.1.call-start = ((), (), s32[]{:S(2)}) async-start(), calls=%async_computation.6 | async-start | bytes 4595712 | tf_op jit(solution)/shard_map/reduce_scatter | solution.py:333
  558.9 41.4 %copy-start.46 = (bf16[512,2,256]{0,2,1:T(8,128)(2,1)S(1)}, bf16[512,2,256]{0,2,1:T(8,128)(2,1)}, u32[]{:S(2)}) copy-start(bf16[512,2,256]{0,2,1:T(8,128)(2,1)} %copy-done.45) | copy-start | bytes 1572868
  558.9 41.4 %copy-start.48 = (bf16[512,2,256]{0,2,1:T(8,128)(2,1)S(1)}, bf16[512,2,256]{0,2,1:T(8,128)(2,1)}, u32[]{:S(2)}) copy-start(bf16[512,2,256]{0,2,1:T(8,128)(2,1)} %copy.680) | copy-start | bytes 1572868
  558.9 41.4 %copy-start.50 = (bf16[512,2,256]{0,2,1:T(8,128)(2,1)S(1)}, bf16[512,2,256]{0,2,1:T(8,128)(2,1)}, u32[]{:S(2)}) copy-start(bf16[512,2,256]{0,2,1:T(8,128)(2,1)} %copy.679) | copy-start | bytes 1572868
  558.9 41.5 %copy-start.65 = (bf16[8,768,64]{1,2,0:T(8,128)(2,1)S(1)}, bf16[8,768,64]{1,2,0:T(8,128)(2,1)}, u32[]{:S(2)}) copy-start(bf16[8,768,64]{1,2,0:T(8,128)(2,1)} %convolution_convert_fusion.7) | copy-start | bytes 2359300
  558.9 41.5 %copy-start.67 = (bf16[8,768,64]{1,2,0:T(8,128)(2,1)S(1)}, bf16[8,768,64]{1,2,0:T(8,128)(2,1)}, u32[]{:S(2)}) copy-start(bf16[8,768,64]{1,2,0:T(8,128)(2,1)} %copy-done.66) | copy-start | bytes 2359300
  611.7 6.6 copy-start.35
  613.0 6.9 copy-start.20
  613.0 6.9 copy-start.22
  613.0 6.9 copy-start.88
  613.0 6.9 copy-start.92
  613.0 6.9 copy-start.105
  613.0 6.9 copy-start.204
  670.2 14.5 %collective-permute-start.1 = (bf16[384,512]{0,1:T(8,128)(2,1)S(1)}, bf16[384,512]{0,1:T(8,128)(2,1)S(1)}, u32[]{:S(2)}, u32[]{:S(2)}) collective-permute-start(bf16[384,512]{0,1:T(8,128)(2,1)S(1)} %select_convert_fusion.1), channel_id=1, source_target_pairs={{0,1},{1,0},{2,3},{3,2},{4,5},{5,4},{6,7},{7,6},{8,9},{9,8},{10,11... | collective-permute-start | bytes 1179656 | tf_op jit(solution)/shard_map/ppermute | solution.py:129
  670.9 13.7 %copy-start.25 = (f32[768,512]{0,1:T(8,128)S(1)}, f32[768,512]{0,1:T(8,128)}, u32[]{:S(2)}) copy-start(f32[768,512]{0,1:T(8,128)} %get-tuple-element.181) | copy-start | bytes 4718596
  672.9 11.9 %copy-start.23 = (f32[768,512]{0,1:T(8,128)}, f32[768,512]{0,1:T(8,128)S(1)}, u32[]{:S(2)}) copy-start(f32[768,512]{0,1:T(8,128)S(1)} %fusion.25) | copy-start | bytes 4718596
  673.0 21.1 %collective-permute-start.3 = (bf16[384,512]{0,1:T(8,128)(2,1)S(1)}, bf16[384,512]{0,1:T(8,128)(2,1)}, u32[]{:S(2)}, u32[]{:S(2)}) collective-permute-start(bf16[384,512]{0,1:T(8,128)(2,1)S(1)} %select_convert_fusion), channel_id=1, source_target_pairs={{0,1},{1,0},{2,3},{3,2},{4,5},{5,4},{6,7},{7,6},{8,9},{9,8},{10,11... | collective-permute-start | bytes 1179656 | tf_op jit(solution)/shard_map/ppermute | solution.py:129
  684.9 9.2 %copy-start.24 = (f32[768,512]{0,1:T(8,128)S(1)}, f32[768,512]{0,1:T(8,128)}, u32[]{:S(2)}) copy-start(f32[768,512]{0,1:T(8,128)} %copy-done.23) | copy-start | bytes 4718596
  735.9 144.6 %copy-start.197 = (f32[6,32,256]{2,1,0:T(8,128)}, f32[6,32,256]{2,1,0:T(8,128)S(1)}, u32[]{:S(2)}) copy-start(f32[6,32,256]{2,1,0:T(8,128)S(1)} %constant_dynamic-update-slice_fusion.18) | copy-start | bytes 589828
  (165 other events, 464.6 us)
Sparse Core Ops, SparseCore 0:
  13.9 65.3 all-gather.9
  82.7 60.6 all-gather.11
  146.8 61.5 all-gather.7
  456.1 138.6 reduce-scatter.5
  596.9 137.9 reduce-scatter.7
  737.0 138.4 reduce-scatter.3

commit v2 on v1

--- a/solution.py
+++ b/solution.py
@@ -53,6 +53,14 @@
 def swish_slope(values):
     sigmoid = jax.nn.sigmoid(values)
     return sigmoid * (1.0 + values * (1.0 - sigmoid))
+
+
+def stack_rows(rows):
+    place = lax.broadcasted_iota(jnp.int32, (len(rows), rows[0].shape[0]), 0)
+    stacked = jnp.zeros(place.shape, single)
+    for index, row in enumerate(rows):
+        stacked = jnp.where(place == index, row[None, :], stacked)
+    return stacked
 
 
 def depthwise(gated, taps):
@@ -80,7 +88,7 @@
         grad_taps.append(
             jnp.sum(padded[:, tap_index : tap_index + length, :] * grad_convolved, axis=(0, 1))
         )
-    return (grad_gated, jnp.stack(grad_taps))
+    return (grad_gated, stack_rows(grad_taps))
 
 
 def per_device(
@@ -155,9 +163,49 @@
         spacing = [(0, 0)] * (flat.ndim - 1) + [(0, depth * LANES - flat.shape[-1])]
         return jnp.pad(flat, spacing).reshape(flat.shape[:-1] + (depth, LANES))
 
-    def gather(parts):
-        block = jnp.concatenate(parts, axis=1)
+    def gather(block):
         return lax.all_gather(block, EVERY, axis=0, tiled=True).reshape(mp, D, -1)
+
+    dp_bits = list(range(dp.bit_length() - 1))
+    mp_bits = list(range(mp.bit_length() - 1))
+    exchanges = (
+        [("dp", bit) for bit in dp_bits[:2]]
+        + [("mp", bit) for bit in mp_bits]
+        + [("dp", bit) for bit in dp_bits[2:]]
+    )
+    sizes = {"dp": dp, "mp": mp}
+
+    def partner(values, axis, bit):
+        return lax.ppermute(values, axis, [(i, i ^ (1 << bit)) for i in range(sizes[axis])])
+
+    def own_bit(axis, bit):
+        return (lax.axis_index(axis) >> bit) & 1
+
+    def gather_by_pairs(block):
+        held = block[None, None]
+        for axis, bit in reversed(exchanges):
+            other = partner(held, axis, bit)
+            low = own_bit(axis, bit) == 0
+            where = 1 if axis == "mp" else 2
+            pair = [jnp.where(low, held, other), jnp.where(low, other, held)]
+            shape = list(held.shape)
+            shape[where - 1] *= 2
+            held = jnp.stack(pair, axis=where).reshape(shape)
+        return held.reshape(mp, D, -1)
+
+    def sum_by_pairs(blocks):
+        held = blocks.reshape(mp, dp, depth, -1)
+        for axis, bit in exchanges:
+            shape = list(held.shape)
+            where = 0 if axis == "mp" else 1
+            shape[where : where + 1] = [shape[where] // 2, 2]
+            split = held.reshape(shape)
+            choice = own_bit(axis, bit)
+            sent = lax.dynamic_index_in_dim(split, 1 - choice, axis=where + 1, keepdims=False)
+            kept = lax.dynamic_index_in_dim(split, choice, axis=where + 1, keepdims=False)
+            other = partner(sent, axis, bit)
+            held = (kept.astype(single) + other.astype(single)).astype(bfloat)
+        return held.reshape(depth, -1)
 
     def unpack(packed, first, width):
         part = packed[:, :, first : first + width]
@@ -165,9 +213,12 @@
 
     hidden_width = FF // mp
     width = D // mp
-    packed = gather([pair_in[0], pair_out[0], fold(small.reshape(-1))])
-    in_zero = unpack(packed, 0, hidden_width)
-    out_zero = unpack(packed, hidden_width, hidden_width)
+    packed = gather(
+        jnp.concatenate([pair_in[0], pair_out[0], fold(small.reshape(-1))], axis=1)
+    )
+    packed_zero = packed
+    in_zero = packed[:, :, :hidden_width]
+    out_zero = packed[:, :, hidden_width : 2 * hidden_width]
     small_all = (
         packed[:, :, 2 * hidden_width :]
         .reshape(owners, depth * LANES)[:, : small_rows * own]
@@ -187,33 +238,37 @@
     norm_bias = norm_rows_all[1] + norm_rows_all[3]
     taps, affine, biases = channel[:KERNEL], channel[KERNEL : KERNEL + 2], channel[KERNEL + 2 :]
 
-    packed = gather(
-        [in_mats[0, k] for k in range(6)] + [attn_out[0].T, conv_out[0].T]
+    packed = gather_by_pairs(
+        jnp.concatenate(
+            [in_mats[0, k] for k in range(6)] + [attn_out[0].T, conv_out[0].T], axis=1
+        )
     )
     mats = [unpack(packed, k * width, width) for k in range(8)]
     w_position, w_attn, w_conv = (mats[3], mats[6], mats[7])
     w_query = jnp.concatenate(mats[0:3], axis=1)
     w_gate = jnp.concatenate(mats[4:6], axis=1)
-    packed = gather([pair_in[1], pair_out[1]])
-    in_one = unpack(packed, 0, hidden_width)
-    out_one = unpack(packed, hidden_width, hidden_width)
+    block_one = jnp.concatenate([pair_in[1], pair_out[1]], axis=1)
+    block_one, _ = lax.optimization_barrier((block_one, packed_zero))
+    packed = gather(block_one)
+    in_one = packed[:, :, :hidden_width]
+    out_one = packed[:, :, hidden_width:]
 
     def norm_input(values, slot):
         normed, kept = norm_rows(values, norm_gain[slot], norm_bias[slot])
         return (normed.astype(bfloat), kept)
 
     def ff_forward(rows, w_first, w_second):
-        hidden_pre = dot("gd,df->gf", rows, w_first)
+        hidden_pre = dot("gd,mdf->mgf", rows, w_first)
         hidden = jax.nn.silu(hidden_pre).astype(bfloat)
-        return (dot("gf,df->gd", hidden, w_second), (hidden_pre, hidden))
+        return (dot("mgf,mdf->gd", hidden, w_second), (hidden_pre, hidden))
 
     def ff_backward(grad_out, rows, kept, w_first, w_second):
         hidden_pre, hidden = kept
-        grad_second = dot("gd,gf->df", grad_out, hidden)
-        grad_hidden = dot("gd,df->gf", grad_out, w_second)
+        grad_second = dot("gd,mgf->mdf", grad_out, hidden)
+        grad_hidden = dot("gd,mdf->mgf", grad_out, w_second)
         grad_pre = (grad_hidden * swish_slope(hidden_pre)).astype(bfloat)
-        grad_first = dot("gd,gf->df", rows, grad_pre)
-        return (dot("gf,df->gd", grad_pre, w_first), grad_first, grad_second)
+        grad_first = dot("gd,mgf->mdf", rows, grad_pre)
+        return (dot("mgf,mdf->gd", grad_pre, w_first), grad_first, grad_second)
 
     sine, cosine = sinusoids(LENGTH, D)
     angle_rows = jnp.concatenate([cosine, sine], axis=1).astype(bfloat)
@@ -323,13 +378,15 @@
 
     counts = (me < micro).astype(single)
 
-    def scatter(parts):
-        blocks = [
-            jnp.swapaxes(part.astype(bfloat).reshape(D, mp, -1), 0, 1) for part in parts[0]
-        ] + parts[1]
-        block = jnp.concatenate(blocks, axis=2)
+    def by_model(part):
+        return jnp.swapaxes(part.reshape(D, mp, -1), 0, 1)
+
+    def scatter(parts, pairs=True):
+        block = jnp.concatenate([part.astype(bfloat) for part in parts], axis=2)
         if mp != micro:
             block = block * counts.astype(bfloat)
+        if pairs:
+            return sum_by_pairs(block).astype(single)
         return lax.psum_scatter(
             block.reshape(mp * D, -1), EVERY, scatter_dimension=0, tiled=True
         ).astype(single)
@@ -340,7 +397,7 @@
     grad_rows, first_one, second_one = ff_backward(
         (0.5 * grad_four).astype(bfloat), rows_four, ff_second, in_one, out_one
     )
-    owned_one = scatter(([first_one, second_one], []))
+    owned_one = scatter([first_one, second_one], pairs=False)
     grad_norm, gains[3], shifts[3] = norm_rows_back(grad_rows, norm_four, norm_gain[3])
     grad_three = grad_four + grad_norm
     grad_out = grad_three.astype(bfloat)
@@ -374,11 +431,11 @@
         grad_two.astype(bfloat), rows_two, attn_kept
     )
     owned_mats = scatter(
-        (
-            [grad_query[:, k * D : (k + 1) * D] for k in range(3)]
-            + [grad_position, grad_gate[:, :D], grad_gate[:, D:], grad_attn, grad_conv],
-            [],
-        )
+        [by_model(grad_query[:, k * D : (k + 1) * D]) for k in range(3)]
+        + [
+            by_model(part)
+            for part in (grad_position, grad_gate[:, :D], grad_gate[:, D:], grad_attn, grad_conv)
+        ]
     )
     grad_norm, gains[1], shifts[1] = norm_rows_back(grad_rows, norm_two, norm_gain[1])
     grad_one = grad_two + grad_norm
@@ -392,11 +449,11 @@
     )
     channel_grads = jnp.swapaxes(channel_grads.reshape(channel_rows, owners, own), 0, 1)
     norm_grads = (
-        jnp.stack(gains + shifts).reshape(10, dp, mp, own).transpose(2, 1, 0, 3)
+        stack_rows(gains + shifts).reshape(10, dp, mp, own).transpose(2, 1, 0, 3)
     ).reshape(owners, 10, own)
     small_grads = jnp.concatenate([channel_grads, norm_grads], axis=1).reshape(owners, -1)
     owned_zero = scatter(
-        ([first_zero, second_zero], [fold(small_grads.astype(bfloat)).reshape(mp, D, LANES)])
+        [first_zero, second_zero, fold(small_grads).reshape(mp, D, LANES)]
     )
     owned_small = owned_zero[:, 2 * hidden_width :].reshape(-1)[: (channel_rows + 10) * own]
     owned_small = owned_small.reshape(1, channel_rows + 10, own)

time: 900 us -> 651 us (0.72)
  waiting for transfers between devices: 338 us -> 115 us
  local copies, waits for them, and re-layouts: 251 us -> 195 us
  other arithmetic: 95.9 us -> 121 us
  starting transfers between devices: 5.37 us -> 18.4 us
    reduce_scatter x3 -> x1, waiting for transfers between devices: 176 us -> 0.02 us  [scatter(): lax.psum_scatter(block.reshape(mp * D, -1), EVERY, scatter_dimension=0, t...]
    all_gather x3 -> x2, waiting for transfers between devices: 133 us -> 0.02 us  [gather(): return lax.all_gather(block, EVERY, axis=0, tiled=True).reshape(mp, D, -1)]
    ppermute x0 -> x15, waiting for transfers between devices: none -> 115 us  [partner(): lax.ppermute(values, axis, [(i, i ^ 1 << bit) for i in range(sizes[axis])])]
    concatenate x34 -> x4, local copies, waits for them, and re-layouts: 54.5 us -> 1.52 us  [per_device(): jnp.concatenate([grad_taps, jnp.stack([local_scale, local_shift]), grad_b...]
    broadcast_in_dim x0 -> x92, local copies, waits for them, and re-layouts: none -> 40.2 us  [stack_rows(): stacked = jnp.where(place == index, row[None, :], stacked)]
    reshape x13 -> x1, local copies, waits for them, and re-layouts: 32.9 us -> 0.09 us  [per_device(): small.reshape(-1)]
    transpose x15 -> x9, local copies, waits for them, and re-layouts: 40.4 us -> 13.1 us  [unpack(): return jnp.swapaxes(part, 0, 1).reshape(D, mp * width)]
    ppermute x2, waiting for transfers between devices: 17.8 us -> 0.01 us  [leave(): other = lax.ppermute(sent, 'mp', swap).astype(single)]
  transfers between devices with their start and end apart: 10 -> 22, of which waited for: 9 -> 10; matrix products, arithmetic and copies ran while one was open for 30% -> 44% of each run, Pallas kernels for 0% -> 0%
where the time goes in v2:
time: 651 us; the launch traced here: 641 us
  local copies, waits for them, and re-layouts  195 us (30%)
  matrix products  135 us (21%)
  other arithmetic  121 us (19%)
  waiting for transfers between devices  115 us (18%)
  blocking collectives  38.3 us (6%)
  starting transfers between devices  18.4 us (3%)
  between operations  17.2 us (3%)
    dot_general x34, matrix products, dot(): return jnp.einsum(spec, left, right, preferred_element_type=single)  122 us
    ppermute x15, waiting for transfers between devices, partner(): lax.ppermute(values, axis, [(i, i ^ 1 << bit) for i in range(sizes[axis])])  115 us
    broadcast_in_dim x92, local copies, waits for them, and re-layouts, stack_rows(): stacked = jnp.where(place == index, row[None, :], stacked)  40.2 us
    unnamed x506, local copies, waits for them, and re-layouts  37 us
    all_gather x1, blocking collectives, per_device(): lax.all_gather(jnp.stack([local_center, jnp.sum(local_offset * local_offs...  20.7 us
    mul x31, local copies, waits for them, and re-layouts, depthwise(): taps[tap_index] * padded[:, tap_index:tap_index + length, :]  20.2 us
    concatenate x3, local copies, waits for them, and re-layouts, scatter(): block = jnp.concatenate([part.astype(bfloat) for part in parts], axis=2)  19.4 us
    all_gather x1, blocking collectives, per_device(): lax.all_gather(jnp.stack([local_shift, local_scale]), 'dp', axis=0)  17.6 us
  transfers between devices with their start and end apart: 22, of which 10 were waited for; matrix products, arithmetic and copies ran while one was open for 44% of the time, Pallas kernels for 0%

profile of v2, /device:TPU:0, one launch (start us, length us, event | category | flops | bytes accessed | tf_op | source)
XLA Modules:
  0.0 641.0 jit_solution(10095795747327965087)
XLA Ops:
  24.7 4.0 collective-permute-start.1
  34.4 3.4 collective-permute-done.1
  40.7 7.9 %collective-permute-done.2 = bf16[1,2,32,2048]{3,2,1,0:T(8,128)(2,1)S(1)} collective-permute-done((bf16[1,2,32,2048]{3,2,1,0:T(8,128)(2,1)S(1)}, bf16[1,2,32,2048]{3,2,1,0:T(8,128)(2,1)S(1)}, u32[]{:S(2)}, u32[]{:S(2)}) %collective-permute-start.2) | collective-permute-done | bytes 262176 | tf_op jit(solution)/shard_map/ppermute | solution.py:179
  53.0 9.4 %collective-permute-done.3 = bf16[1,4,32,2048]{3,2,1,0:T(8,128)(2,1)S(1)} collective-permute-done((bf16[1,4,32,2048]{3,2,1,0:T(8,128)(2,1)S(1)}, bf16[1,4,32,2048]{3,2,1,0:T(8,128)(2,1)S(1)}, u32[]{:S(2)}, u32[]{:S(2)}) %collective-permute-start.3) | collective-permute-done | bytes 524320 | tf_op jit(solution)/shard_map/ppermute | solution.py:179
  70.7 24.0 %collective-permute-done.4 = bf16[2,4,32,2048]{3,2,1,0:T(8,128)(2,1)} collective-permute-done((bf16[2,4,32,2048]{3,2,1,0:T(8,128)(2,1)}, bf16[2,4,32,2048]{3,2,1,0:T(8,128)(2,1)}, u32[]{:S(2)}, u32[]{:S(2)}) %collective-permute-start.4) | collective-permute-done | bytes 1048608 | tf_op jit(solution)/shard_map/ppermute | solution.py:179
  98.3 3.8 fusion.151
  109.6 2.5 select_bitcast_fusion.1
  156.4 6.7 %fusion.16 = (bf16[2,768,1024]{1,2,0:T(8,128)(2,1)S(1)}, f32[2,1024,768]{2,1,0:T(8,128)}) fusion(f32[512]{0:T(512)S(1)} %bitcast.800, f32[512]{0:T(512)S(1)} %bitcast.767, f32[768]{0:T(1024)S(1)} %add_rsqrt_fusion.4, f32[768]{0:T(1024)S(1)} %broadcast_multiply_fusion.14, bf16[384,512]{0,1:T(8,128)(2,1)S(1)} %get-tuple-element.176, ...), kind=kOutput, calls=%fused_computation.29 | convolution fusion | flops 1622016000 | bytes 12331008 | tf_op jit(solution)/shard_map/gd,mdf->mgf/dot_general | solution.py:23
  164.7 3.4 fusion.202
  169.3 3.8 fusion.203
  176.1 3.1 multiply_convert_fusion.6
  179.2 2.3 copy.600
  181.5 2.3 copy.604
  183.8 3.3 convolution_bitcast_fusion
  189.3 9.2 %fusion.1 = f32[8,768,768]{1,2,0:T(8,128)} fusion(bf16[8,768,256]{1,2,0:T(8,128)(2,1)S(1)} %get-tuple-element.132, bf16[8,768,256]{1,2,0:T(8,128)(2,1)S(1)} %get-tuple-element.131, bf16[768,256]{1,0:T(8,128)(2,1)S(1)} %copy-done.74, bf16[768,256]{1,0:T(8,128)(2,1)S(1)} %copy-done.72), kind=kOutput, calls=%fused_computation.5 | convolution fusion | flops 4845993984 | bytes 25952256 | tf_op jit(solution)/shard_map/shik,jk->shij/dot_general | solution.py:23
  198.5 13.5 %fusion.204 = (f32[8,768]{1,0:T(8,128)}, f32[8,768,768]{1,2,0:T(8,128)}) fusion(f32[8,768,768]{1,2,0:T(8,128)} %fusion.1, bf16[8,768,64]{1,2,0:T(8,128)(2,1)} %bitcast.710, bf16[8,768,64]{1,2,0:T(8,128)(2,1)S(1)} %bitcast.704), kind=kOutput, calls=%fused_computation.499 | convolution fusion | flops 618136320 | bytes 39346176 | tf_op jit(solution)/shard_map/sub | solution.py:299
  212.0 7.2 %divide_convert_fusion = bf16[8,768,768]{1,2,0:T(8,128)(2,1)S(1)} fusion(f32[8,768,768]{1,2,0:T(8,128)} %get-tuple-element.258, f32[8,768]{1,0:T(8,128)} %get-tuple-element.257), kind=kLoop, calls=%fused_computation.2 | loop fusion | flops 9437184 | bytes 28336128 | tf_op jit(solution)/shard_map/convert_element_type | solution.py:301
  219.2 3.4 fusion.205
  229.3 6.7 %fusion.189 = (f32[512]{0:T(512)S(1)}, f32[1,768,512]{2,1,0:T(8,128)S(1)}) fusion(f32[512]{0:T(512)S(1)} %copy-done.129, f32[512]{0:T(512)S(1)} %copy-done.131, f32[512]{0:T(512)S(1)} %copy-done.133, f32[512]{0:T(512)S(1)} %copy-done.135, f32[512]{0:T(512)S(1)} %copy-done.137, f32[512]{0:T(512)S(1)} %copy-done.139, f32[512]{0:T(512)S(1)} %copy-done.141, ...), kind=kLoop, calls=%fused_computation.485 | loop fusion | flops 25951744 | bytes 6356992 | tf_op jit(solution)/shard_map/reduce_sum | solution.py:358
  236.2 20.7 %all-gather.2 = f32[16,2,512]{2,1,0:T(2,128)S(1)} all-gather(f32[1,2,512]{2,1,0:T(2,128)S(1)} %maximum_bitcast_fusion.8), channel_id=2, replica_groups=mesh['dp'=16,'mp'=2] {'dp'}, dimensions={0}, use_global_device_ids=true | all-gather | bytes 69632 | tf_op jit(solution)/shard_map/all_gather | solution.py:360
  260.1 4.8 fusion.10
  269.4 4.6 fusion.6
  274.1 3.6 fusion.212
  277.6 3.5 convert_bitcast_fusion.1
  281.1 3.5 convert_bitcast_fusion
  284.6 3.1 copy.656
  287.7 3.1 multiply_reduce_fusion.2
  291.0 3.8 multiply_add_fusion.3
  298.7 17.6 %all-gather.3 = f32[16,2,512]{2,1,0:T(2,128)S(1)} all-gather(f32[1,2,512]{2,1,0:T(2,128)S(1)} %maximum_bitcast_fusion.9), channel_id=3, replica_groups=mesh['dp'=16,'mp'=2] {'dp'}, dimensions={0}, use_global_device_ids=true | all-gather | bytes 69632 | tf_op jit(solution)/shard_map/all_gather | solution.py:408
  316.4 4.3 multiply_reduce_fusion.33
  322.1 2.4 multiply_reduce_fusion.14
  324.5 2.5 multiply_reduce_fusion.24
  327.3 6.5 %fusion.70 = (bf16[768,512]{1,0:T(8,128)(2,1)S(1)}, f32[1,768,512]{2,1,0:T(8,128)S(1)}) fusion(f32[768,1024]{1,0:T(8,128)S(1)} %copy-done.3, f32[512]{0:T(512)S(1)} %copy-done.130, f32[512]{0:T(512)S(1)} %copy-done.132, f32[512]{0:T(512)S(1)} %copy-done.134, f32[512]{0:T(512)S(1)} %copy-done.136, f32[512]{0:T(512)S(1)} %copy-done.138, ...), kind=kLoop, calls=%fused_computation.123 | loop fusion | flops 25952256 | bytes 7141376 | tf_op jit(solution)/shard_map/convert_element_type | solution.py:421
  335.4 2.8 fusion.211
  340.2 3.0 copy.658
  343.2 2.7 multiply_reduce_fusion.1
  348.1 8.5 %convolution_convert_fusion.3 = bf16[8,768,64]{1,2,0:T(8,128)(2,1)} fusion(bf16[8,768,768]{1,2,0:T(8,128)(2,1)} %copy-done, bf16[8,768,64]{1,2,0:T(8,128)(2,1)S(1)} %bitcast.697), kind=kOutput, calls=%fused_computation.239 | convolution fusion | flops 604372992 | bytes 11010048 | tf_op jit(solution)/shard_map/shij,shid->shjd/dot_general | solution.py:23
  357.7 5.4 multiply_convert_fusion
  363.1 7.8 %convolution_convert_fusion.4 = bf16[8,768,64]{1,2,0:T(8,128)(2,1)} fusion(bf16[8,768,768]{1,2,0:T(8,128)(2,1)} %multiply_convert_fusion, bf16[8,768,64]{1,2,0:T(8,128)(2,1)} %bitcast.711), kind=kOutput, calls=%fused_computation.240 | convolution fusion | flops 604372992 | bytes 11010048 | tf_op jit(solution)/shard_map/shij,shid->shjd/dot_general | solution.py:23
  370.9 2.4 fusion.213
  373.3 5.6 convolution_bitcast_fusion.1
  380.9 2.9 fusion.119
  388.0 2.7 convolution_convert_fusion
  392.3 2.6 multiply_reduce_fusion
  395.4 6.8 %fusion.5 = bf16[2,768,1024]{1,2,0:T(8,128)(2,1)S(1)} fusion(f32[2,1024,768]{2,1,0:T(8,128)} %get-tuple-element.252, bf16[2,512,2176]{2,1,0:T(8,128)(2,1)} %bitcast.791, f32[768,512]{0,1:T(8,128)S(1)} %multiply_add_fusion), kind=kOutput, calls=%fused_computation.11 | convolution fusion | flops 1625554944 | bytes 13107200 | tf_op jit(solution)/shard_map/gd,mdf->mgf/dot_general | solution.py:23
  402.3 5.2 fusion.209
  407.6 3.4 convert_bitcast_fusion.3
  411.0 3.2 convert_bitcast_fusion.2
  415.9 4.5 pad_maximum_fusion.3
  420.5 6.4 %copy.730 = bf16[2,512,2048]{2,1,0:T(8,128)(2,1)} copy(bf16[2,512,2048]{1,2,0:T(8,128)(2,1)} %pad_maximum_fusion.3) | data formatting | bytes 8388608 | tf_op jit(solution)/shard_map/concatenate | solution.py:385
  435.4 2.3 copy.792
  508.0 6.4 copy.740
  514.4 3.4 dynamic-slice_bitcast_fusion.1
  517.8 2.3 pad_maximum_fusion.1
  520.1 6.6 %copy.725 = bf16[2,512,2176]{2,1,0:T(8,128)(2,1)} copy(bf16[2,512,2176]{1,2,0:T(8,128)(2,1)} %pad_maximum_fusion.1) | data formatting | bytes 8912896 | tf_op jit(solution)/shard_map/concatenate | solution.py:385
  526.8 3.4 dynamic-slice_bitcast_fusion
  535.8 3.2 fusion.20
  547.6 3.0 copy.744
  550.7 21.5 %collective-permute-done.15 = bf16[2,4,32,2048]{3,2,1,0:T(8,128)(2,1)} collective-permute-done((bf16[2,4,32,2048]{3,2,1,0:T(8,128)(2,1)S(1)}, bf16[2,4,32,2048]{3,2,1,0:T(8,128)(2,1)}, u32[]{:S(2)}, u32[]{:S(2)}) %collective-permute-start.15) | collective-permute-done | bytes 1048608 | tf_op jit(solution)/shard_map/ppermute | solution.py:179
  575.4 20.1 %collective-permute-done.10 = bf16[2,4,32,2176]{3,2,1,0:T(8,128)(2,1)} collective-permute-done((bf16[2,4,32,2176]{3,2,1,0:T(8,128)(2,1)}, bf16[2,4,32,2176]{3,2,1,0:T(8,128)(2,1)}, u32[]{:S(2)}, u32[]{:S(2)}) %collective-permute-start.10) | collective-permute-done | bytes 1114144 | tf_op jit(solution)/shard_map/ppermute | solution.py:179
  598.5 12.8 %collective-permute-done.11 = bf16[1,4,32,2176]{3,2,1,0:T(8,128)(2,1)S(1)} collective-permute-done((bf16[1,4,32,2176]{3,2,1,0:T(8,128)(2,1)S(1)}, bf16[1,4,32,2176]{3,2,1,0:T(8,128)(2,1)S(1)}, u32[]{:S(2)}, u32[]{:S(2)}) %collective-permute-start.11) | collective-permute-done | bytes 557088 | tf_op jit(solution)/shard_map/ppermute | solution.py:179
  612.2 5.4 collective-permute-done.18
  618.3 3.6 collective-permute-done.12
  622.1 7.1 %collective-permute-done.13 = bf16[1,1,32,2176]{3,2,1,0:T(8,128)(2,1)S(1)} collective-permute-done((bf16[1,1,32,2176]{3,2,1,0:T(8,128)(2,1)S(1)}, bf16[1,1,32,2176]{3,2,1,0:T(8,128)(2,1)S(1)}, u32[]{:S(2)}, u32[]{:S(2)}) %collective-permute-start.13) | collective-permute-done | bytes 139296 | tf_op jit(solution)/shard_map/ppermute | solution.py:179
  (915 shorter events, 243.0 us)
Async XLA Ops:
  7.2 21.5 %copy-start.62 = (bf16[2,384,512]{2,1,0:T(8,128)(2,1)S(1)}, bf16[2,384,512]{2,1,0:T(8,128)(2,1)}, u32[]{:S(2)}) copy-start(bf16[2,384,512]{2,1,0:T(8,128)(2,1)} %param.12) | copy-start | bytes 2359300
  7.2 119.0 %all-gather.7.cloned.1.call-start = ((), (), s32[]{:S(2)}) async-start(), calls=%async_computation.1 | async-start | bytes 4595712 | tf_op jit(solution)/shard_map/all_gather | solution.py:167
  14.0 246.1 %all-gather.9.cloned.1.call-start = ((), (), s32[]{:S(2)}) async-start(), calls=%async_computation.2 | async-start | bytes 4325376 | tf_op jit(solution)/shard_map/all_gather | solution.py:167
  24.7 13.2 %collective-permute-start.1 = (bf16[1,1,32,2048]{3,2,1,0:T(8,128)(2,1)}, bf16[1,1,32,2048]{3,2,1,0:T(8,128)(2,1)}, u32[]{:S(2)}, u32[]{:S(2)}) collective-permute-start(bf16[1,1,32,2048]{3,2,1,0:T(8,128)(2,1)} %bitcast.30), channel_id=1, source_target_pairs={{0,16},{2,18},{4,20},{6,22},{8,24},{10,26},{12,28},{14,30},{16,0},... | collective-permute-start | bytes 393224 | tf_op jit(solution)/shard_map/ppermute | solution.py:179
  30.0 76.2 %collective-permute-start = (bf16[384,512]{0,1:T(8,128)(2,1)}, bf16[384,512]{0,1:T(8,128)(2,1)}, u32[]{:S(2)}, u32[]{:S(2)}) collective-permute-start(bf16[384,512]{0,1:T(8,128)(2,1)} %bitcast_select_fusion.4), channel_id=1, source_target_pairs={{0,1},{1,0},{2,3},{3,2},{4,5},{5,4},{6,7},{7,6},{8,9},{9,8},{10,11... | collective-permute-start | bytes 1179656 | tf_op jit(solution)/shard_map/ppermute | solution.py:126
  33.9 73.8 %collective-permute-start.7 = (bf16[384,512]{0,1:T(8,128)(2,1)}, bf16[384,512]{0,1:T(8,128)(2,1)}, u32[]{:S(2)}, u32[]{:S(2)}) collective-permute-start(bf16[384,512]{0,1:T(8,128)(2,1)} %bitcast_select_fusion.1), channel_id=1, source_target_pairs={{0,1},{1,0},{2,3},{3,2},{4,5},{5,4},{6,7},{7,6},{8,9},{9,8},{10,11... | collective-permute-start | bytes 1179656 | tf_op jit(solution)/shard_map/ppermute | solution.py:126
  38.9 9.8 %collective-permute-start.2 = (bf16[1,2,32,2048]{3,2,1,0:T(8,128)(2,1)S(1)}, bf16[1,2,32,2048]{3,2,1,0:T(8,128)(2,1)S(1)}, u32[]{:S(2)}, u32[]{:S(2)}) collective-permute-start(bf16[1,2,32,2048]{3,2,1,0:T(8,128)(2,1)S(1)} %maximum_bitcast_fusion.4), channel_id=1, source_target_pairs={{0,8},{2,10},{4,12},{6,14},{8,0},{10,2},{12,4},{14,6},{16,24},{18,... | collective-permute-start | bytes 786440 | tf_op jit(solution)/shard_map/ppermute | solution.py:179
  48.7 13.7 %collective-permute-start.3 = (bf16[1,4,32,2048]{3,2,1,0:T(8,128)(2,1)S(1)}, bf16[1,4,32,2048]{3,2,1,0:T(8,128)(2,1)S(1)}, u32[]{:S(2)}, u32[]{:S(2)}) collective-permute-start(bf16[1,4,32,2048]{3,2,1,0:T(8,128)(2,1)S(1)} %bitcast.725), channel_id=1, source_target_pairs={{0,1},{1,0},{2,3},{3,2},{4,5},{5,4},{6,7},{7,6},{8,9},{9,8},{10,11... | collective-permute-start | bytes 1572872 | tf_op jit(solution)/shard_map/ppermute | solution.py:179
  63.6 31.1 %collective-permute-start.4 = (bf16[2,4,32,2048]{3,2,1,0:T(8,128)(2,1)}, bf16[2,4,32,2048]{3,2,1,0:T(8,128)(2,1)}, u32[]{:S(2)}, u32[]{:S(2)}) collective-permute-start(bf16[2,4,32,2048]{3,2,1,0:T(8,128)(2,1)} %maximum_bitcast_fusion), channel_id=1, source_target_pairs={{0,4},{2,6},{4,0},{6,2},{8,12},{10,14},{12,8},{14,10},{16,20},{18,... | collective-permute-start | bytes 3145736 | tf_op jit(solution)/shard_map/ppermute | solution.py:179
  97.7 11.9 %collective-permute-start.5 = (bf16[2,8,32,2048]{3,2,1,0:T(8,128)(2,1)}, bf16[2,8,32,2048]{3,2,1,0:T(8,128)(2,1)}, u32[]{:S(2)}, u32[]{:S(2)}) collective-permute-start(bf16[2,8,32,2048]{3,2,1,0:T(8,128)(2,1)} %bitcast.43), channel_id=1, source_target_pairs={{0,2},{2,0},{4,6},{6,4},{8,10},{10,8},{12,14},{14,12},{16,18},{18,... | collective-permute-start | bytes 6291464 | tf_op jit(solution)/shard_map/ppermute | solution.py:179
  107.3 55.7 %copy-start.20 = (bf16[384,512]{0,1:T(8,128)(2,1)}, bf16[384,512]{0,1:T(8,128)(2,1)S(1)}, u32[]{:S(2)}) copy-start(bf16[384,512]{0,1:T(8,128)(2,1)S(1)} %get-tuple-element.175) | copy-start | bytes 1179652
  107.3 55.7 %copy-start.22 = (bf16[384,512]{0,1:T(8,128)(2,1)}, bf16[384,512]{0,1:T(8,128)(2,1)S(1)}, u32[]{:S(2)}) copy-start(bf16[384,512]{0,1:T(8,128)(2,1)S(1)} %get-tuple-element.176) | copy-start | bytes 1179652
  107.5 48.9 %copy-start.80 = (f32[768]{0:T(1024)}, f32[768]{0:T(1024)S(1)}, u32[]{:S(2)}) copy-start(f32[768]{0:T(1024)S(1)} %broadcast_multiply_fusion.14) | copy-start | bytes 9220
  107.7 48.6 %copy-start.84 = (f32[768]{0:T(1024)}, f32[768]{0:T(1024)S(1)}, u32[]{:S(2)}) copy-start(f32[768]{0:T(1024)S(1)} %add_rsqrt_fusion.4) | copy-start | bytes 9220
  124.2 44.2 %copy-start.51 = (bf16[512,2,256]{0,2,1:T(8,128)(2,1)}, bf16[512,2,256]{0,2,1:T(8,128)(2,1)S(1)}, u32[]{:S(2)}) copy-start(bf16[512,2,256]{0,2,1:T(8,128)(2,1)S(1)} %copy.598) | copy-start | bytes 1572868
  129.0 502.8 %reduce-scatter.2.cloned.1.call-start = ((), (), s32[]{:S(2)}) async-start(), calls=%async_computation.3 | async-start | bytes 4325376 | tf_op jit(solution)/shard_map/reduce_scatter | solution.py:390
  129.7 98.2 %copy-start.99 = (f32[512]{0:T(512)}, f32[512]{0:T(512)S(1)}, u32[]{:S(2)}) copy-start(f32[512]{0:T(512)S(1)} %mul.1192) | copy-start | bytes 6148
  174.4 24.1 %copy-start.30 = (bf16[768,512]{0,1:T(8,128)(2,1)}, bf16[768,512]{0,1:T(8,128)(2,1)S(1)}, u32[]{:S(2)}) copy-start(bf16[768,512]{0,1:T(8,128)(2,1)S(1)} %copy.601) | copy-start | bytes 2359300
  176.1 43.1 %copy-start.32 = (bf16[768,512]{0,1:T(8,128)(2,1)}, bf16[768,512]{0,1:T(8,128)(2,1)S(1)}, u32[]{:S(2)}) copy-start(bf16[768,512]{0,1:T(8,128)(2,1)S(1)} %copy.608) | copy-start | bytes 2359300
  224.2 33.6 %copy-start.4 = (f32[768,512]{0,1:T(8,128)}, f32[768,512]{0,1:T(8,128)S(1)}, u32[]{:S(2)}) copy-start(f32[768,512]{0,1:T(8,128)S(1)} %get-tuple-element.262) | copy-start | bytes 4718596
  235.9 22.8 %copy-start.6 = (f32[1,768,512]{2,1,0:T(8,128)}, f32[1,768,512]{2,1,0:T(8,128)S(1)}, u32[]{:S(2)}) copy-start(f32[1,768,512]{2,1,0:T(8,128)S(1)} %get-tuple-element.128) | copy-start | bytes 4718596
  235.9 21.2 %copy-start.185 = (f32[1,512]{1,0:T(1,128)S(1)}, f32[1,512]{1,0:T(1,128)}, u32[]{:S(2)}) copy-start(f32[1,512]{1,0:T(1,128)} %slice.833) | copy-start | bytes 6148
  235.9 21.8 %copy-start.70 = (bf16[512,2,256]{0,2,1:T(8,128)(2,1)S(1)}, bf16[512,2,256]{0,2,1:T(8,128)(2,1)}, u32[]{:S(2)}) copy-start(bf16[512,2,256]{0,2,1:T(8,128)(2,1)} %copy.646) | copy-start | bytes 1572868
  236.0 21.8 %copy-start.178 = (f32[512]{0:T(512)S(1)}, f32[512]{0:T(512)}, u32[]{:S(2)}) copy-start(f32[512]{0:T(512)} %mul.1298) | copy-start | bytes 6148
  236.0 21.8 %copy-start.180 = (f32[512]{0:T(512)S(1)}, f32[512]{0:T(512)}, u32[]{:S(2)}) copy-start(f32[512]{0:T(512)} %add.573) | copy-start | bytes 6148
  266.8 14.3 %copy-start.15 = (f32[768,512]{0,1:T(8,128)}, f32[768,512]{0,1:T(8,128)S(1)}, u32[]{:S(2)}) copy-start(f32[768,512]{0,1:T(8,128)S(1)} %get-tuple-element.268) | copy-start | bytes 4718596
  267.1 14.0 %copy-start.86 = (f32[768]{0:T(1024)}, f32[768]{0:T(1024)S(1)}, u32[]{:S(2)}) copy-start(f32[768]{0:T(1024)S(1)} %add_rsqrt_fusion) | copy-start | bytes 9220
  296.0 20.4 %copy-start.92 = (f32[512]{0:T(512)S(1)}, f32[512]{0:T(512)}, u32[]{:S(2)}) copy-start(f32[512]{0:T(512)} %copy-done.90) | copy-start | bytes 6148
  296.0 20.4 %copy-start.95 = (f32[512]{0:T(512)S(1)}, f32[512]{0:T(512)}, u32[]{:S(2)}) copy-start(f32[512]{0:T(512)} %copy-done.93) | copy-start | bytes 6148
  296.0 20.4 %copy-start.177 = (f32[1,512]{1,0:T(1,128)S(1)}, f32[1,512]{1,0:T(1,128)}, u32[]{:S(2)}) copy-start(f32[1,512]{1,0:T(1,128)} %mul.1330) | copy-start | bytes 6148
  395.4 15.6 %copy-start.42 = (f32[768,512]{0,1:T(8,128)}, f32[768,512]{0,1:T(8,128)S(1)}, u32[]{:S(2)}) copy-start(f32[768,512]{0,1:T(8,128)S(1)} %multiply_add_fusion) | copy-start | bytes 4718596
  433.6 13.2 %copy-start.209 = (bf16[512]{0:T(512)(128)(2,1)S(1)}, bf16[512]{0:T(512)(128)(2,1)}, u32[]{:S(2)}) copy-start(bf16[512]{0:T(512)(128)(2,1)} %get-tuple-element.87) | copy-start | bytes 3076
  433.6 14.0 %copy-start.207 = (bf16[512]{0:T(512)(128)(2,1)S(1)}, bf16[512]{0:T(512)(128)(2,1)}, u32[]{:S(2)}) copy-start(bf16[512]{0:T(512)(128)(2,1)} %get-tuple-element.88) | copy-start | bytes 3076
  433.6 14.7 %copy-start.211 = (bf16[512]{0:T(512)(128)(2,1)S(1)}, bf16[512]{0:T(512)(128)(2,1)}, u32[]{:S(2)}) copy-start(bf16[512]{0:T(512)(128)(2,1)} %get-tuple-element.98) | copy-start | bytes 3076
  433.6 15.5 %copy-start.215 = (bf16[512]{0:T(512)(128)(2,1)S(1)}, bf16[512]{0:T(512)(128)(2,1)}, u32[]{:S(2)}) copy-start(bf16[512]{0:T(512)(128)(2,1)} %get-tuple-element.89) | copy-start | bytes 3076
  433.6 16.2 %copy-start.208 = (bf16[512]{0:T(512)(128)(2,1)S(1)}, bf16[512]{0:T(512)(128)(2,1)}, u32[]{:S(2)}) copy-start(bf16[512]{0:T(512)(128)(2,1)} %get-tuple-element.99) | copy-start | bytes 3076
  433.7 17.0 %copy-start.206 = (bf16[512]{0:T(512)(128)(2,1)S(1)}, bf16[512]{0:T(512)(128)(2,1)}, u32[]{:S(2)}) copy-start(bf16[512]{0:T(512)(128)(2,1)} %get-tuple-element.100) | copy-start | bytes 3076
  433.7 17.7 %copy-start.205 = (bf16[512]{0:T(512)(128)(2,1)S(1)}, bf16[512]{0:T(512)(128)(2,1)}, u32[]{:S(2)}) copy-start(bf16[512]{0:T(512)(128)(2,1)} %get-tuple-element.101) | copy-start | bytes 3076
  433.7 18.5 %copy-start.204 = (bf16[512]{0:T(512)(128)(2,1)S(1)}, bf16[512]{0:T(512)(128)(2,1)}, u32[]{:S(2)}) copy-start(bf16[512]{0:T(512)(128)(2,1)} %get-tuple-element.102) | copy-start | bytes 3076
  433.7 19.3 %copy-start.203 = (bf16[512]{0:T(512)(128)(2,1)S(1)}, bf16[512]{0:T(512)(128)(2,1)}, u32[]{:S(2)}) copy-start(bf16[512]{0:T(512)(128)(2,1)} %get-tuple-element.103) | copy-start | bytes 3076
  433.7 20.0 %copy-start.202 = (bf16[512]{0:T(512)(128)(2,1)S(1)}, bf16[512]{0:T(512)(128)(2,1)}, u32[]{:S(2)}) copy-start(bf16[512]{0:T(512)(128)(2,1)} %get-tuple-element.104) | copy-start | bytes 3076
  433.7 20.8 %copy-start.201 = (bf16[512]{0:T(512)(128)(2,1)S(1)}, bf16[512]{0:T(512)(128)(2,1)}, u32[]{:S(2)}) copy-start(bf16[512]{0:T(512)(128)(2,1)} %get-tuple-element.105) | copy-start | bytes 3076
  433.7 21.5 %copy-start.200 = (bf16[512]{0:T(512)(128)(2,1)S(1)}, bf16[512]{0:T(512)(128)(2,1)}, u32[]{:S(2)}) copy-start(bf16[512]{0:T(512)(128)(2,1)} %get-tuple-element.106) | copy-start | bytes 3076
  433.7 22.3 %copy-start.199 = (bf16[512]{0:T(512)(128)(2,1)S(1)}, bf16[512]{0:T(512)(128)(2,1)}, u32[]{:S(2)}) copy-start(bf16[512]{0:T(512)(128)(2,1)} %get-tuple-element.90) | copy-start | bytes 3076
  433.7 23.0 %copy-start.198 = (bf16[512]{0:T(512)(128)(2,1)S(1)}, bf16[512]{0:T(512)(128)(2,1)}, u32[]{:S(2)}) copy-start(bf16[512]{0:T(512)(128)(2,1)} %get-tuple-element.91) | copy-start | bytes 3076
  433.7 23.8 %copy-start.197 = (bf16[512]{0:T(512)(128)(2,1)S(1)}, bf16[512]{0:T(512)(128)(2,1)}, u32[]{:S(2)}) copy-start(bf16[512]{0:T(512)(128)(2,1)} %get-tuple-element.92) | copy-start | bytes 3076
  433.8 24.5 %copy-start.196 = (bf16[512]{0:T(512)(128)(2,1)S(1)}, bf16[512]{0:T(512)(128)(2,1)}, u32[]{:S(2)}) copy-start(bf16[512]{0:T(512)(128)(2,1)} %get-tuple-element.93) | copy-start | bytes 3076
  433.8 25.3 %copy-start.195 = (bf16[512]{0:T(512)(128)(2,1)S(1)}, bf16[512]{0:T(512)(128)(2,1)}, u32[]{:S(2)}) copy-start(bf16[512]{0:T(512)(128)(2,1)} %get-tuple-element.94) | copy-start | bytes 3076
  433.8 26.1 %copy-start.194 = (bf16[512]{0:T(512)(128)(2,1)S(1)}, bf16[512]{0:T(512)(128)(2,1)}, u32[]{:S(2)}) copy-start(bf16[512]{0:T(512)(128)(2,1)} %get-tuple-element.95) | copy-start | bytes 3076
  433.8 26.8 %copy-start.193 = (bf16[512]{0:T(512)(128)(2,1)S(1)}, bf16[512]{0:T(512)(128)(2,1)}, u32[]{:S(2)}) copy-start(bf16[512]{0:T(512)(128)(2,1)} %get-tuple-element.96) | copy-start | bytes 3076
  433.8 27.6 %copy-start.192 = (bf16[512]{0:T(512)(128)(2,1)S(1)}, bf16[512]{0:T(512)(128)(2,1)}, u32[]{:S(2)}) copy-start(bf16[512]{0:T(512)(128)(2,1)} %get-tuple-element.97) | copy-start | bytes 3076
  433.8 28.3 %copy-start.223 = (bf16[512]{0:T(512)(128)(2,1)S(1)}, bf16[512]{0:T(512)(128)(2,1)}, u32[]{:S(2)}) copy-start(bf16[512]{0:T(512)(128)(2,1)} %get-tuple-element.145) | copy-start | bytes 3076
  433.8 99.0 %collective-permute-start.6 = (bf16[384,512]{0,1:T(8,128)(2,1)}, bf16[384,512]{0,1:T(8,128)(2,1)}, u32[]{:S(2)}, u32[]{:S(2)}) collective-permute-start(bf16[384,512]{0,1:T(8,128)(2,1)} %select_convert_fusion.1), channel_id=1, source_target_pairs={{0,1},{1,0},{2,3},{3,2},{4,5},{5,4},{6,7},{7,6},{8,9},{9,8},{10,11... | collective-permute-start | bytes 1179656 | tf_op jit(solution)/shard_map/ppermute | solution.py:137
  517.8 18.0 %collective-permute-start.14 = (bf16[2,8,32,2048]{3,2,1,0:T(8,128)(2,1)}, bf16[2,8,32,2048]{3,2,1,0:T(8,128)(2,1)}, u32[]{:S(2)}, u32[]{:S(2)}) collective-permute-start(bf16[2,8,32,2048]{3,2,1,0:T(8,128)(2,1)} %dynamic-slice_bitcast_fusion.1), channel_id=1, source_target_pairs={{0,2},{2,0},{4,6},{6,4},{8,10},{10,8},{12,14},{14,12},{16,18},{18,... | collective-permute-start | bytes 6291464 | tf_op jit(solution)/shard_map/ppermute | solution.py:179
  530.2 10.6 %collective-permute-start.9 = (bf16[2,8,32,2176]{3,2,1,0:T(8,128)(2,1)}, bf16[2,8,32,2176]{3,2,1,0:T(8,128)(2,1)}, u32[]{:S(2)}, u32[]{:S(2)}) collective-permute-start(bf16[2,8,32,2176]{3,2,1,0:T(8,128)(2,1)} %dynamic-slice_bitcast_fusion), channel_id=1, source_target_pairs={{0,2},{2,0},{4,6},{6,4},{8,10},{10,8},{12,14},{14,12},{16,18},{18,... | collective-permute-start | bytes 6684680 | tf_op jit(solution)/shard_map/ppermute | solution.py:179
  532.3 13.0 %collective-permute-start.8 = (bf16[384,512]{0,1:T(8,128)(2,1)}, bf16[384,512]{0,1:T(8,128)(2,1)}, u32[]{:S(2)}, u32[]{:S(2)}) collective-permute-start(bf16[384,512]{0,1:T(8,128)(2,1)} %select_convert_fusion), channel_id=1, source_target_pairs={{0,1},{1,0},{2,3},{3,2},{4,5},{5,4},{6,7},{7,6},{8,9},{9,8},{10,11... | collective-permute-start | bytes 1179656 | tf_op jit(solution)/shard_map/ppermute | solution.py:137
  539.1 33.1 %collective-permute-start.15 = (bf16[2,4,32,2048]{3,2,1,0:T(8,128)(2,1)S(1)}, bf16[2,4,32,2048]{3,2,1,0:T(8,128)(2,1)}, u32[]{:S(2)}, u32[]{:S(2)}) collective-permute-start(bf16[2,4,32,2048]{3,2,1,0:T(8,128)(2,1)S(1)} %dynamic-slice_bitcast_fusion.3), channel_id=1, source_target_pairs={{0,4},{2,6},{4,0},{6,2},{8,12},{10,14},{12,8},{14,10},{16,20},{18,... | collective-permute-start | bytes 3145736 | tf_op jit(solution)/shard_map/ppermute | solution.py:179
  544.2 51.4 %collective-permute-start.10 = (bf16[2,4,32,2176]{3,2,1,0:T(8,128)(2,1)}, bf16[2,4,32,2176]{3,2,1,0:T(8,128)(2,1)}, u32[]{:S(2)}, u32[]{:S(2)}) collective-permute-start(bf16[2,4,32,2176]{3,2,1,0:T(8,128)(2,1)} %dynamic-slice_bitcast_fusion.2), channel_id=1, source_target_pairs={{0,4},{2,6},{4,0},{6,2},{8,12},{10,14},{12,8},{14,10},{16,20},{18,... | collective-permute-start | bytes 3342344 | tf_op jit(solution)/shard_map/ppermute | solution.py:179
  574.1 24.1 %collective-permute-start.16 = (bf16[1,4,32,2048]{3,2,1,0:T(8,128)(2,1)S(1)}, bf16[1,4,32,2048]{3,2,1,0:T(8,128)(2,1)S(1)}, u32[]{:S(2)}, u32[]{:S(2)}) collective-permute-start(bf16[1,4,32,2048]{3,2,1,0:T(8,128)(2,1)S(1)} %constant_dynamic-slice_fusion.1), channel_id=1, source_target_pairs={{0,1},{1,0},{2,3},{3,2},{4,5},{5,4},{6,7},{7,6},{8,9},{9,8},{10,11... | collective-permute-start | bytes 1572872 | tf_op jit(solution)/shard_map/ppermute | solution.py:179
  597.1 14.2 %collective-permute-start.11 = (bf16[1,4,32,2176]{3,2,1,0:T(8,128)(2,1)S(1)}, bf16[1,4,32,2176]{3,2,1,0:T(8,128)(2,1)S(1)}, u32[]{:S(2)}, u32[]{:S(2)}) collective-permute-start(bf16[1,4,32,2176]{3,2,1,0:T(8,128)(2,1)S(1)} %constant_dynamic-slice_fusion.3), channel_id=1, source_target_pairs={{0,1},{1,0},{2,3},{3,2},{4,5},{5,4},{6,7},{7,6},{8,9},{9,8},{10,11... | collective-permute-start | bytes 1671176 | tf_op jit(solution)/shard_map/ppermute | solution.py:179
  598.4 13.1 %collective-permute-start.17 = (bf16[1,2,32,2048]{3,2,1,0:T(8,128)(2,1)S(1)}, bf16[1,2,32,2048]{3,2,1,0:T(8,128)(2,1)S(1)}, u32[]{:S(2)}, u32[]{:S(2)}) collective-permute-start(bf16[1,2,32,2048]{3,2,1,0:T(8,128)(2,1)S(1)} %dynamic-slice_bitcast_fusion.5), channel_id=1, source_target_pairs={{0,8},{2,10},{4,12},{6,14},{8,0},{10,2},{12,4},{14,6},{16,24},{18,... | collective-permute-start | bytes 786440 | tf_op jit(solution)/shard_map/ppermute | solution.py:179
  611.6 6.0 collective-permute-start.18
  611.7 10.2 %collective-permute-start.12 = (bf16[1,2,32,2176]{3,2,1,0:T(8,128)(2,1)S(1)}, bf16[1,2,32,2176]{3,2,1,0:T(8,128)(2,1)S(1)}, u32[]{:S(2)}, u32[]{:S(2)}) collective-permute-start(bf16[1,2,32,2176]{3,2,1,0:T(8,128)(2,1)S(1)} %dynamic-slice_bitcast_fusion.4), channel_id=1, source_target_pairs={{0,8},{2,10},{4,12},{6,14},{8,0},{10,2},{12,4},{14,6},{16,24},{18,... | collective-permute-start | bytes 835592 | tf_op jit(solution)/shard_map/ppermute | solution.py:179
  622.0 7.2 %collective-permute-start.13 = (bf16[1,1,32,2176]{3,2,1,0:T(8,128)(2,1)S(1)}, bf16[1,1,32,2176]{3,2,1,0:T(8,128)(2,1)S(1)}, u32[]{:S(2)}, u32[]{:S(2)}) collective-permute-start(bf16[1,1,32,2176]{3,2,1,0:T(8,128)(2,1)S(1)} %constant_dynamic-slice_fusion.2), channel_id=1, source_target_pairs={{0,16},{2,18},{4,20},{6,22},{8,24},{10,26},{12,28},{14,30},{16,0},... | collective-permute-start | bytes 417800 | tf_op jit(solution)/shard_map/ppermute | solution.py:179
  (197 other events, 774.4 us)
Sparse Core Ops, SparseCore 0:
  14.1 75.5 all-gather.6
  129.1 62.2 all-gather.8
  427.0 139.8 reduce-scatter.1
